TPU v7x, 32 devices: a whole 2x2x4 slice. The times are simulated.
32 devices in a mesh: dp: 16 (over z, y, x), tensor: 2 (over core).
Axes of the slice: x: 2, y: 2, z: 4, core: 2. Of those that a mesh axis runs over, the one named last changes fastest.
Arguments:
- tokens: bfloat16 [16384, 768], P('dp'), may hold values from -6 to 6
- segments: int32 [16, 1024], P('dp'), may hold values from 0 to 7, never falling along the last dimension, each value on 1 to 512 neighbouring positions
- gain_attn: float32 [768], replicated, may hold values from 0.5 to 1.5
- w_qkv: bfloat16 [768, 3, 768], P(None, None, 'tensor'), may hold values from -0.21875 to 0.21875
- w_attn_out: bfloat16 [768, 768], P('tensor'), may hold values from -1.75 to 1.75
- bias_table: float32 [32, 12], P(None, 'tensor'), may hold values from -4 to 4
- gain_ffn: float32 [768], replicated, may hold values from 0.5 to 1.5
- router: float32 [768, 16], replicated, may hold values from -0.15625 to 0.15625
- expert_in: bfloat16 [16, 768, 3072], P('dp', None, 'tensor'), may hold values from -0.21875 to 0.21875
- expert_out: bfloat16 [16, 3072, 768], P('dp', 'tensor'), may hold values from -4 to 4
- expert_ids: int32 [16384, 1], P('dp'), may hold values from 0 to 15; in each aligned block of 1024 rows (0 to 1023, 1024 to 2047, ...) at most 128 rows name the same one
- cotangent: bfloat16 [16384, 768], P('dp'), may hold values from -21 to 21
Outputs:
- output: bfloat16 [16384, 768], P('dp')
- grad_tokens: float32 [16384, 768], P('dp')
- grad_gain_attn: float32 [768], replicated
- grad_w_qkv: float32 [768, 3, 768], P(None, None, 'tensor')
- grad_w_attn_out: float32 [768, 768], P('tensor')
- grad_bias_table: float32 [32, 12], P(None, 'tensor')
- grad_gain_ffn: float32 [768], replicated
- grad_router: float32 [768, 16], replicated
- grad_expert_in: float32 [16, 768, 3072], P('dp', None, 'tensor')
- grad_expert_out: float32 [16, 3072, 768], P('dp', 'tensor')
Inputs may be any that keep to these rules, and one draw needn't show every extreme that they name: `segments`: within each sequence the document numbers never fall, and each document holds at most 512 positions. `expert_ids`: among the 1024 tokens of one sequence no expert is chosen more than 128 times, and some expert is chosen exactly 128 times.
All inputs are finite; a program needn't handle non-finite values.
Results may differ from a plain program's by a relative error of at most 0.013.
The roundings to bfloat16 on the way count: a program that leaves them out, or rounds other values in their place, can miss the bound.
Values may be sent and summed in bfloat16 or wider, within the bound.
A program may use at most 192 MiB of HBM per device.

v0:
```python
import jax
import jax.numpy as jnp
from jax import lax
from jax.sharding import PartitionSpec as P

epsilon = 1e-06
highest = lax.Precision.HIGHEST
bucket_edges = (8, 12, 16, 23, 32, 46, 64, 91)


def bucket_ids(row_positions, col_positions, half_count):
    offset = col_positions[None, :] - row_positions[:, None]
    distance = jnp.abs(offset)
    far_part = jnp.zeros_like(distance)
    for edge_value in bucket_edges:
        far_part = far_part + (distance >= edge_value).astype(jnp.int32)
    near_far = jnp.where(distance < 8, distance, 7 + far_part)
    return near_far + half_count * (offset > 0).astype(jnp.int32)


def bias_from_table(table_t, bucket):
    bias_sum = jnp.zeros((table_t.shape[0],) + bucket.shape, jnp.float32)
    for bucket_number in range(table_t.shape[1]):
        column = table_t[:, bucket_number][:, None, None]
        bias_sum = bias_sum + jnp.where(bucket[None] == bucket_number, column, 0.0)
    return bias_sum


def table_from_grads(grad_scores, bucket, bucket_count):
    columns = []
    for bucket_number in range(bucket_count):
        masked = jnp.where(bucket[None] == bucket_number, grad_scores, 0.0)
        columns.append(jnp.sum(masked, axis=(1, 2)))
    return jnp.stack(columns, axis=1)


def gelu_tanh(inner_act):
    return jax.nn.gelu(inner_act, approximate=True)


def heads_total(partial_sum):
    return lax.psum(partial_sum, "tensor")


def to_owners(buffer, model_width):
    grouped = buffer.reshape(lax.axis_size("dp"), -1, model_width)
    arrived = lax.all_to_all(grouped, "dp", split_axis=0, concat_axis=0, tiled=True)
    return arrived


def to_senders(partial_rows, model_width):
    summed = lax.psum(partial_rows, "tensor")
    arrived = lax.all_to_all(
        summed.astype(jnp.bfloat16), "dp", split_axis=0, concat_axis=0, tiled=True
    )
    return arrived.reshape(-1, model_width)


def per_device(
    tokens,
    segments,
    gain_attn,
    w_qkv,
    w_attn_out,
    bias_table,
    gain_ffn,
    router,
    expert_in,
    expert_out,
    expert_ids,
    cotangent,
):
    length, model_width = tokens.shape
    head_cols = w_qkv.shape[2]
    heads_here = bias_table.shape[1]
    head_size = head_cols // heads_here
    experts_all = router.shape[1]
    experts_here = expert_in.shape[0]
    capacity = max(2, 2 * length // experts_all)
    block_rows = min(512, length)
    block_count = length // block_rows
    segment_row = segments[0]
    table_t = bias_table.T
    bucket_count = bias_table.shape[0]
    half_count = bucket_count // 2
    col_positions = jnp.arange(length, dtype=jnp.int32)
    inputs32 = tokens.astype(jnp.float32)
    scale_one = lax.rsqrt(jnp.mean(inputs32 * inputs32, axis=1, keepdims=True) + epsilon)
    normed_one = inputs32 * scale_one
    normed = (normed_one * gain_attn).astype(jnp.bfloat16)
    w_flat = w_qkv.reshape(model_width, 3 * head_cols)
    packed = jnp.dot(normed, w_flat, preferred_element_type=jnp.float32).astype(jnp.bfloat16)
    packed = packed.reshape(length, 3, heads_here, head_size)
    queries = packed[:, 0]
    keys_all = packed[:, 1]
    values_all = packed[:, 2]

    def score_block(row_start):
        row_positions = row_start + jnp.arange(block_rows, dtype=jnp.int32)
        query_block = lax.dynamic_slice_in_dim(queries, row_start, block_rows, 0)
        seg_block = lax.dynamic_slice_in_dim(segment_row, row_start, block_rows, 0)
        raw_scores = (
            jnp.einsum("qhd,khd->hqk", query_block, keys_all, preferred_element_type=jnp.float32)
            * 0.125
        )
        bucket = bucket_ids(row_positions, col_positions, half_count)
        same_doc = seg_block[:, None] == segment_row[None, :]
        return (raw_scores, bucket, same_doc, query_block)

    def forward_block(block_index):
        raw_scores, bucket, same_doc, query_block = score_block(block_index * block_rows)
        scores = jnp.where(same_doc[None], raw_scores + bias_from_table(table_t, bucket), -1e30)
        row_peak = jnp.max(scores, axis=2, keepdims=True)
        shifted = jnp.exp(scores - row_peak)
        row_total = jnp.sum(shifted, axis=2, keepdims=True)
        weights = (shifted / row_total).astype(jnp.bfloat16)
        attended = jnp.einsum(
            "hqk,khd->qhd", weights, values_all, preferred_element_type=jnp.float32
        )
        return (attended, (row_peak + jnp.log(row_total))[:, :, 0])

    attended, log_norm = lax.map(forward_block, jnp.arange(block_count, dtype=jnp.int32))
    mixed_heads = attended.reshape(length, head_cols).astype(jnp.bfloat16)
    attn_part = jnp.dot(mixed_heads, w_attn_out, preferred_element_type=jnp.float32)
    hidden = inputs32 + heads_total(attn_part)
    scale_two = lax.rsqrt(jnp.mean(hidden * hidden, axis=1, keepdims=True) + epsilon)
    normed_two = hidden * scale_two
    ffn_in = normed_two * gain_ffn
    router_logits = jnp.dot(ffn_in, router, precision=highest)
    logit_peak = jnp.max(router_logits, axis=1, keepdims=True)
    router_exp = jnp.exp(router_logits - logit_peak)
    router_probs = router_exp / jnp.sum(router_exp, axis=1, keepdims=True)
    chosen = expert_ids[:, 0]
    one_hot_int = (chosen[:, None] == jnp.arange(experts_all, dtype=jnp.int32)[None, :]).astype(
        jnp.int32
    )
    one_hot_float = one_hot_int.astype(jnp.float32)
    gate_prob = jnp.sum(router_probs * one_hot_float, axis=1)
    slot_ids = jnp.sum((jnp.cumsum(one_hot_int, axis=0) - one_hot_int) * one_hot_int, axis=1)
    target_rows = chosen * capacity + slot_ids
    send_buffer = (
        jnp.zeros((experts_all * capacity, model_width), jnp.bfloat16)
        .at[target_rows]
        .set(ffn_in.astype(jnp.bfloat16))
    )
    expert_rows = to_owners(send_buffer, model_width).reshape(
        -1, experts_here, capacity, model_width
    )
    inner_act = jnp.einsum(
        "secd,edf->secf", expert_rows, expert_in, preferred_element_type=jnp.float32
    )
    activated, gelu_back = jax.vjp(gelu_tanh, inner_act)
    act_low = activated.astype(jnp.bfloat16)
    expert_part = jnp.einsum(
        "secf,efd->secd", act_low, expert_out, preferred_element_type=jnp.float32
    )
    returned = to_senders(expert_part.reshape(lax.axis_size("dp"), -1, model_width), model_width)
    picked = returned[target_rows].astype(jnp.float32)
    output = (hidden + gate_prob[:, None] * picked).astype(jnp.bfloat16)
    upstream = cotangent.astype(jnp.float32)
    grad_gate = jnp.sum(upstream * picked, axis=1)
    back_rows = (gate_prob[:, None] * upstream).astype(jnp.bfloat16)
    back_buffer = (
        jnp.zeros((experts_all * capacity, model_width), jnp.bfloat16)
        .at[target_rows]
        .set(back_rows)
    )
    expert_grads = to_owners(back_buffer, model_width).reshape(
        -1, experts_here, capacity, model_width
    )
    grad_act = jnp.einsum(
        "secd,efd->secf", expert_grads, expert_out, preferred_element_type=jnp.float32
    )
    grad_inner = gelu_back(grad_act)[0].astype(jnp.bfloat16)
    grad_expert_out = jnp.einsum(
        "secf,secd->efd", act_low, expert_grads, preferred_element_type=jnp.float32
    )
    grad_expert_in = jnp.einsum(
        "secd,secf->edf", expert_rows, grad_inner, preferred_element_type=jnp.float32
    )
    grad_rows = jnp.einsum(
        "secf,edf->secd", grad_inner, expert_in, preferred_element_type=jnp.float32
    )
    grad_sent = to_senders(grad_rows.reshape(lax.axis_size("dp"), -1, model_width), model_width)[
        target_rows
    ].astype(jnp.float32)
    grad_logits = router_probs * (one_hot_float - gate_prob[:, None]) * grad_gate[:, None]
    grad_router = jnp.dot(ffn_in.T, grad_logits, precision=highest)
    grad_ffn_in = grad_sent + jnp.dot(grad_logits, router.T, precision=highest)
    grad_gain_ffn = jnp.sum(grad_ffn_in * normed_two, axis=0)
    grad_norm_two = grad_ffn_in * gain_ffn
    grad_hidden = upstream + scale_two * (
        grad_norm_two - normed_two * jnp.mean(grad_norm_two * normed_two, axis=1, keepdims=True)
    )
    grad_attn = grad_hidden.astype(jnp.bfloat16)
    grad_w_attn_out = jnp.dot(mixed_heads.T, grad_attn, preferred_element_type=jnp.float32)
    grad_mixed = jnp.dot(grad_attn, w_attn_out.T, preferred_element_type=jnp.float32).astype(
        jnp.bfloat16
    )
    grad_mixed = grad_mixed.reshape(length, heads_here, head_size)

    def backward_block(carry, block_index):
        grad_keys, grad_values, grad_table = carry
        row_start = block_index * block_rows
        raw_scores, bucket, same_doc, query_block = score_block(row_start)
        scores = jnp.where(same_doc[None], raw_scores + bias_from_table(table_t, bucket), -1e30)
        probs_block = jnp.exp(scores - log_norm[block_index][:, :, None])
        out_grad = lax.dynamic_slice_in_dim(grad_mixed, row_start, block_rows, 0)
        grad_probs = jnp.einsum(
            "qhd,khd->hqk", out_grad, values_all, preferred_element_type=jnp.float32
        )
        row_dot = jnp.sum(probs_block * grad_probs, axis=2, keepdims=True)
        grad_scores = probs_block * (grad_probs - row_dot)
        grad_table = grad_table + table_from_grads(grad_scores, bucket, bucket_count)
        low_scores = grad_scores.astype(jnp.bfloat16)
        grad_query = (
            jnp.einsum("hqk,khd->qhd", low_scores, keys_all, preferred_element_type=jnp.float32)
            * 0.125
        )
        grad_keys = (
            grad_keys
            + jnp.einsum(
                "hqk,qhd->khd", low_scores, query_block, preferred_element_type=jnp.float32
            )
            * 0.125
        )
        grad_values = grad_values + jnp.einsum(
            "hqk,qhd->khd",
            probs_block.astype(jnp.bfloat16),
            out_grad,
            preferred_element_type=jnp.float32,
        )
        return ((grad_keys, grad_values, grad_table), grad_query)

    zero_heads = jnp.zeros((length, heads_here, head_size), jnp.float32)
    start_carry = (zero_heads, zero_heads, jnp.zeros(table_t.shape, jnp.float32))
    final_carry, grad_queries = lax.scan(
        backward_block, start_carry, jnp.arange(block_count, dtype=jnp.int32)
    )
    grad_keys, grad_values, grad_table = final_carry
    grad_queries = grad_queries.reshape(length, heads_here, head_size)
    grad_packed = (
        jnp.stack([grad_queries, grad_keys, grad_values], axis=1)
        .astype(jnp.bfloat16)
        .reshape(length, 3 * head_cols)
    )
    grad_w_qkv = jnp.dot(normed.T, grad_packed, preferred_element_type=jnp.float32).reshape(
        model_width, 3, head_cols
    )
    grad_normed = heads_total(jnp.dot(grad_packed, w_flat.T, preferred_element_type=jnp.float32))
    grad_gain_attn = jnp.sum(grad_normed * normed_one, axis=0)
    grad_norm_one = grad_normed * gain_attn
    grad_tokens = grad_hidden + scale_one * (
        grad_norm_one - normed_one * jnp.mean(grad_norm_one * normed_one, axis=1, keepdims=True)
    )
    summed = lax.psum(
        (grad_gain_attn, grad_w_qkv, grad_w_attn_out, grad_table.T, grad_gain_ffn, grad_router),
        "dp",
    )
    return (
        output,
        grad_tokens,
        summed[0],
        summed[1],
        summed[2],
        summed[3],
        summed[4],
        summed[5],
        grad_expert_in,
        grad_expert_out,
    )


def solution(mesh):
    return jax.shard_map(
        per_device,
        mesh=mesh,
        in_specs=(
            P("dp", None),
            P("dp", None),
            P(),
            P(None, None, "tensor"),
            P("tensor", None),
            P(None, "tensor"),
            P(),
            P(),
            P("dp", None, "tensor"),
            P("dp", "tensor", None),
            P("dp", None),
            P("dp", None),
        ),
        out_specs=(
            P("dp", None),
            P("dp", None),
            P(),
            P(None, None, "tensor"),
            P("tensor", None),
            P(None, "tensor"),
            P(),
            P(),
            P("dp", None, "tensor"),
            P("dp", "tensor", None),
        ),
        check_vma=False,
    )
```

profile of v0, /device:TPU:12, one launch (start us, length us, event | category | flops | bytes accessed | tf_op | source)
XLA Modules:
  0.0 1215.3 jit_solution(6210028493848861521)
XLA Ops:
  27.5 155.9 %while.30 = (s32[]{:T(128)}, bf16[2,512,6,64]{1,3,2,0:T(8,128)(2,1)}, f32[2,6,512]{2,1,0:T(8,128)}, s32[2]{0:T(128)S(1)}, s32[1024]{0:T(1024)S(1)}, /*index=5*/s...) while((s32[]{:T(128)}, ...), condition=%wide.region_4.5_spmd.clone, body=%wide.region_1.4_spmd.clone.sunk | while | flops 1065350656 | bytes 81744616 | solution.py:122
  32.4 13.4 %broadcast_compare_fusion.70 = (pred[512,1024]{1,0:T(8,128)(4,1)S(1)}, pred[512,1024]{1,0:T(8,128)(4,1)S(1)}, pred[512,1024]{1,0:T(8,128)(4,1)S(1)}, pred[512,10...) fusion(s32[512]{0:T(512)S(1)} %iota_add_fusion.4), kind=kLoop, calls=%fused_computation.52.clone.1 | loop fusion | flops 33030144 | bytes 16779264 | tf_op jit(solution)/shard_map/while/body/eval_jaxpr/eq | solution.py:25
  45.9 51.3 %fusion.198 = (f32[6,512]{1,0:T(8,128)S(1)}, f32[6,512,1024]{2,1,0:T(8,128)S(1)}) fusion(f32[6]{0:T(128)S(1)} %get-tuple-element.755, pred[512,1024]{1,0:T(8,128)(4,1)} %get-tuple-element.756, f32[6]{0:T(128)S(1)} %get-tuple-element.757, pred[512,1024]{1,0:T(8,128)(4,1)} %get-tuple-element.758, f32[6]{0:T(128)S(1)} %get-tuple-element.759, ...), kind=kOutput, calls=%fused_computation.353.clone.1 | convolution fusion | flops 613413888 | bytes 31077124 | tf_op jit(solution)/shard_map/while/body/eval_jaxpr/qhd,khd->hqk/dot_general | solution.py:103
  110.1 13.4 %broadcast_compare_fusion.70 = (pred[512,1024]{1,0:T(8,128)(4,1)S(1)}, pred[512,1024]{1,0:T(8,128)(4,1)S(1)}, pred[512,1024]{1,0:T(8,128)(4,1)S(1)}, pred[512,10...) fusion(s32[512]{0:T(512)S(1)} %iota_add_fusion.4), kind=kLoop, calls=%fused_computation.52.clone.1 | loop fusion | flops 33030144 | bytes 16779264 | tf_op jit(solution)/shard_map/while/body/eval_jaxpr/eq | solution.py:25
  123.5 51.3 %fusion.198 = (f32[6,512]{1,0:T(8,128)S(1)}, f32[6,512,1024]{2,1,0:T(8,128)S(1)}) fusion(f32[6]{0:T(128)S(1)} %get-tuple-element.755, pred[512,1024]{1,0:T(8,128)(4,1)} %get-tuple-element.756, f32[6]{0:T(128)S(1)} %get-tuple-element.757, pred[512,1024]{1,0:T(8,128)(4,1)} %get-tuple-element.758, f32[6]{0:T(128)S(1)} %get-tuple-element.759, ...), kind=kOutput, calls=%fused_computation.353.clone.1 | convolution fusion | flops 613413888 | bytes 31077124 | tf_op jit(solution)/shard_map/while/body/eval_jaxpr/qhd,khd->hqk/dot_general | solution.py:103
  194.2 19.7 %all-reduce.8.cloned.1.call-done = f32[1024,768]{1,0:T(8,128)} async-done(((f32[1024,768]{1,0:T(8,128)}), f32[1024,768]{1,0:T(8,128)}) %all-reduce.8.cloned.1.call-update) | async-done | bytes 3145744 | tf_op jit(solution)/shard_map/psum | solution.py:42
  218.3 8.5 scatter_custom_fusion
  239.0 8.2 scatter_custom_fusion.1
  247.2 58.3 %all-to-all-done = bf16[16,128,768]{2,1,0:T(8,128)(2,1)} async-done(((bf16[16,128,768]{2,1,0:T(8,128)(2,1)}), bf16[16,128,768]{2,1,0:T(8,128)(2,1)}, u32[]{:S(2)}, u32[]{:S(2)}) %all-to-all-start) | async-done | bytes 3145760 | tf_op jit(solution)/shard_map/all_to_all | solution.py:47
  324.2 9.2 fusion.74
  333.5 48.2 %all-to-all-done.2 = bf16[16,128,768]{2,1,0:T(8,128)(2,1)} async-done(((bf16[16,128,768]{2,1,0:T(8,128)(2,1)}), bf16[16,128,768]{2,1,0:T(8,128)(2,1)}, u32[]{:S(2)}, u32[]{:S(2)}) %all-to-all-start.2) | async-done | bytes 3145760 | tf_op jit(solution)/shard_map/all_to_all | solution.py:47
  381.7 15.9 %fusion.63 = bf16[16,1,128,1536]{3,2,0,1:T(8,128)(2,1)S(1)} fusion(f32[16,128,1536]{2,1,0:T(8,128)} %copy-done.80, bf16[16,128,768]{2,1,0:T(8,128)(2,1)} %all-to-all-done.2, bf16[1,1536,768]{2,1,0:T(8,128)(2,1)S(1)} %copy-done), kind=kOutput, calls=%fused_computation.238 | convolution fusion | flops 4894752768 | bytes 24379392 | tf_op jit(solution)/shard_map/secd,efd->secf/dot_general | solution.py:171
  407.6 35.8 %all-reduce.13 = (bf16[16,128,768]{2,1,0:T(8,128)(2,1)}, bf16[16,128,768]{2,1,0:T(8,128)(2,1)}) all-reduce(f32[16,128,768]{2,1,0:T(8,128)} %fusion.74, f32[16,128,768]{2,1,0:T(8,128)} %fusion.70), channel_id=1, replica_groups=mesh['dp'=16,'tensor'=2] {'tensor'}, use_global_device_ids=true, to_apply=%region_14.15 | all-reduce | flops 3145728 | bytes 18874368 | tf_op jit(solution)/shard_map/psum | solution.py:52
  443.4 75.6 %all_to_all.20 = bf16[16,128,768]{2,1,0:T(8,128)(2,1)} all-to-all(bf16[16,128,768]{2,1,0:T(8,128)(2,1)} %get-tuple-element.313), channel_id=1, replica_groups=mesh['dp'=16,'tensor'=2] {'dp'}, dimensions={0} | all-to-all | bytes 6291456 | tf_op jit(solution)/shard_map/all_to_all | solution.py:53
  534.8 59.4 %all-to-all-done.3 = bf16[16,128,768]{2,1,0:T(8,128)(2,1)} async-done(((bf16[16,128,768]{2,1,0:T(8,128)(2,1)}), bf16[16,128,768]{2,1,0:T(8,128)(2,1)}, u32[]{:S(2)}, u32[]{:S(2)}) %all-to-all-start.3) | async-done | bytes 3145760 | tf_op jit(solution)/shard_map/all_to_all | solution.py:53
  613.9 370.1 %while.31 = (s32[]{:T(128)}, f32[1024,6,64]{0,2,1:T(8,128)}, f32[1024,6,64]{0,2,1:T(8,128)S(1)}, f32[6,32]{1,0:T(8,128)S(1)}, bf16[2,512,6,64]{1,0,3,2:T(2,128)(...) while((s32[]{:T(128)}, f32[1024,6,64]{0,2,1:T(8,128)}, ...), condition=%wide.region_53.54_spmd.clone, body=%wide.region_19.53_spmd.clone.sunk | while | flops 2483287552 | bytes 352014304 | solution.py:237
  628.0 13.5 %broadcast_compare_fusion.72 = (pred[512,1024]{1,0:T(8,128)(4,1)S(1)}, pred[512,1024]{1,0:T(8,128)(4,1)S(1)}, pred[512,1024]{1,0:T(8,128)(4,1)S(1)}, pred[512,10...) fusion(s32[512]{0:T(512)S(1)} %iota_add_fusion.5), kind=kLoop, calls=%fused_computation.179.clone.1 | loop fusion | flops 33030144 | bytes 16779264 | tf_op jit(solution)/shard_map/while/body/eval_jaxpr/eq | solution.py:25
  641.6 56.2 %multiply_reduce_fusion.5 = (f32[6,512]{1,0:T(8,128)S(1)}, f32[6,512,1024]{2,1,0:T(8,128)}) fusion(f32[6,512,1024]{2,1,0:T(8,128)} %fusion.210, f32[6,512]{1,0:T(8,128)S(1)} %dynamic-slice_bitcast_fusion.2, f32[6]{0:T(128)S(1)} %get-tuple-element.853, pred[512,1024]{1,0:T(8,128)(4,1)S(1)} %get-tuple-element.835, f32[6]{0:T(128)S(1)} %get-tuple-element.854, ...), kind=kOutput, calls=%fused_computation.128.clone.1 | convolution fusion | flops 619705344 | bytes 43672324 | tf_op jit(solution)/shard_map/while/body/eval_jaxpr/qhd,khd->hqk/dot_general | solution.py:103
  698.0 36.1 %select_reduce_fusion.34 = (f32[6]{0:T(128)S(1)}, f32[6]{0:T(128)S(1)}, f32[6]{0:T(128)S(1)}, f32[6]{0:T(128)S(1)}, f32[6]{0:T(128)S(1)}, /*index=5*/f32[6]{0:T(...) fusion(pred[512,1024]{1,0:T(8,128)(4,1)} %copy-done.14, ...), kind=kLoop, calls=%fused_computation.95.clone.1 | loop fusion | flops 119537528 | bytes 47198640 | tf_op jit(solution)/shard_map/while/body/eval_jaxpr/reduce_sum | solution.py:33
  734.2 10.7 bitcast_add_fusion.5
  745.4 24.0 %select_reduce_fusion.35 = (f32[6]{0:T(128)S(1)}, f32[6]{0:T(128)S(1)}, f32[6]{0:T(128)S(1)}, f32[6]{0:T(128)S(1)}, f32[6]{0:T(128)S(1)}, /*index=5*/f32[6]{0:T(...) fusion(f32[6,512,1024]{2,1,0:T(8,128)S(1)} %get-tuple-element.9, ...), kind=kLoop, calls=%fused_computation.113.clone.1 | loop fusion | flops 88080280 | bytes 19923280 | tf_op jit(solution)/shard_map/while/body/eval_jaxpr/reduce_sum | solution.py:33
  784.0 14.1 %dynamic_update_slice.21 = bf16[2,512,6,64]{1,0,3,2:T(2,128)(2,1)} dynamic-update-slice(bf16[2,512,6,64]{1,0,3,2:T(2,128)(2,1)} %get-tuple-element.999, bf16[1,512,6,64]{1,0,3,2:T(2,128)(2,1)S(1)} %copy.168, s32[]{:T(128)S(6)} %copy.189, s32[]{:T(128)} %constant.38.clone.1..sunk.1, s32[]{:T(128)} %constant.38.clone.1..sunk.1, s32[]{:T(128)} %constant.38.clone.1..sunk.1) | dynamic-update-slice | bytes 786436 | tf_op jit(solution)/shard_map/while/body/jit(dynamic_update_index_in_dim)/dynamic_update_slice | solution.py:122
  812.0 13.5 %broadcast_compare_fusion.72 = (pred[512,1024]{1,0:T(8,128)(4,1)S(1)}, pred[512,1024]{1,0:T(8,128)(4,1)S(1)}, pred[512,1024]{1,0:T(8,128)(4,1)S(1)}, pred[512,10...) fusion(s32[512]{0:T(512)S(1)} %iota_add_fusion.5), kind=kLoop, calls=%fused_computation.179.clone.1 | loop fusion | flops 33030144 | bytes 16779264 | tf_op jit(solution)/shard_map/while/body/eval_jaxpr/eq | solution.py:25
  825.6 56.2 %multiply_reduce_fusion.5 = (f32[6,512]{1,0:T(8,128)S(1)}, f32[6,512,1024]{2,1,0:T(8,128)}) fusion(f32[6,512,1024]{2,1,0:T(8,128)} %fusion.210, f32[6,512]{1,0:T(8,128)S(1)} %dynamic-slice_bitcast_fusion.2, f32[6]{0:T(128)S(1)} %get-tuple-element.853, pred[512,1024]{1,0:T(8,128)(4,1)S(1)} %get-tuple-element.835, f32[6]{0:T(128)S(1)} %get-tuple-element.854, ...), kind=kOutput, calls=%fused_computation.128.clone.1 | convolution fusion | flops 619705344 | bytes 43672324 | tf_op jit(solution)/shard_map/while/body/eval_jaxpr/qhd,khd->hqk/dot_general | solution.py:103
  882.0 36.1 %select_reduce_fusion.34 = (f32[6]{0:T(128)S(1)}, f32[6]{0:T(128)S(1)}, f32[6]{0:T(128)S(1)}, f32[6]{0:T(128)S(1)}, f32[6]{0:T(128)S(1)}, /*index=5*/f32[6]{0:T(...) fusion(pred[512,1024]{1,0:T(8,128)(4,1)} %copy-done.14, ...), kind=kLoop, calls=%fused_computation.95.clone.1 | loop fusion | flops 119537528 | bytes 47198640 | tf_op jit(solution)/shard_map/while/body/eval_jaxpr/reduce_sum | solution.py:33
  918.2 10.7 bitcast_add_fusion.5
  929.4 24.0 %select_reduce_fusion.35 = (f32[6]{0:T(128)S(1)}, f32[6]{0:T(128)S(1)}, f32[6]{0:T(128)S(1)}, f32[6]{0:T(128)S(1)}, f32[6]{0:T(128)S(1)}, /*index=5*/f32[6]{0:T(...) fusion(f32[6,512,1024]{2,1,0:T(8,128)S(1)} %get-tuple-element.9, ...), kind=kLoop, calls=%fused_computation.113.clone.1 | loop fusion | flops 88080280 | bytes 19923280 | tf_op jit(solution)/shard_map/while/body/eval_jaxpr/reduce_sum | solution.py:33
  969.5 14.1 %dynamic_update_slice.21 = bf16[2,512,6,64]{1,0,3,2:T(2,128)(2,1)} dynamic-update-slice(bf16[2,512,6,64]{1,0,3,2:T(2,128)(2,1)} %get-tuple-element.999, bf16[1,512,6,64]{1,0,3,2:T(2,128)(2,1)S(1)} %copy.168, s32[]{:T(128)S(6)} %copy.189, s32[]{:T(128)} %constant.38.clone.1..sunk.1, s32[]{:T(128)} %constant.38.clone.1..sunk.1, s32[]{:T(128)} %constant.38.clone.1..sunk.1) | dynamic-update-slice | bytes 786436 | tf_op jit(solution)/shard_map/while/body/jit(dynamic_update_index_in_dim)/dynamic_update_slice | solution.py:122
  1003.3 9.8 fusion.83
  1013.2 12.2 %fusion.80 = f32[1,1536,768]{2,1,0:T(8,128)} fusion(bf16[16,128,768]{2,1,0:T(8,128)(2,1)} %all-to-all-done.2, f32[16,128,1536]{2,1,0:T(8,128)} %copy-done.80), kind=kOutput, calls=%fused_computation.266 | convolution fusion | flops 4860149760 | bytes 20447232 | tf_op jit(solution)/shard_map/secf,secd->efd/dot_general | solution.py:175
  1030.5 68.8 %all-reduce = (f32[768]{0:T(1024)}, f32[32,6]{0,1:T(8,128)}, f32[768]{0:T(1024)}, f32[768,16]{0,1:T(8,128)}) all-reduce(f32[768]{0:T(1024)S(1)} %get-tuple-element.257, f32[32,6]{0,1:T(8,128)S(1)} %bitcast.451, f32[768]{0:T(1024)S(1)} %copy-done.73, f32[768,16]{0,1:T(8,128)S(1)} %fusion.97), channel_id=1, replica_groups=mesh['dp'=16,'tensor'=2] {'dp'}, use_global_device_ids=true, to_apply=%region_57.58 | all-reduce | flops 14016 | bytes 112128 | tf_op jit(solution)/shard_map/psum | solution.py:256
  1104.8 98.6 %all-reduce.12.cloned.1.call-done = (f32[768,3,384]{2,0,1:T(8,128)}, f32[384,768]{1,0:T(8,128)}) async-done(((f32[768,3,384]{2,0,1:T(8,128)}, f32[384,768]{1,0:T(8,128)}), (f32[768,3,384]{2,0,1:T(8,128)}, f32[384,768]{1,0:T(8,128)})) %all-reduce.12.cloned.1.call-update) | async-done | bytes 4718608 | tf_op jit(solution)/shard_map/psum | solution.py:256
  (410 shorter events, 224.8 us)
Async XLA Ops:
  7.2 317.1 %copy-start = (bf16[1,1536,768]{2,1,0:T(8,128)(2,1)S(1)}, bf16[1,1536,768]{2,1,0:T(8,128)(2,1)}, u32[]{:S(2)}) copy-start(bf16[1,1536,768]{2,1,0:T(8,128)(2,1)} %param.25) | copy-start | bytes 7077892
  7.2 206.7 %all-reduce.8.cloned.1.call-start = ((), (), s32[]{:S(2)}) async-start(), calls=%async_computation.4 | async-start | bytes 6291456 | tf_op jit(solution)/shard_map/psum | solution.py:42
  218.3 390.0 %copy-start.59 = (f32[1024]{0:T(1024)}, f32[1024]{0:T(1024)S(1)}, u32[]{:S(2)}) copy-start(f32[1024]{0:T(1024)S(1)} %add_rsqrt_fusion) | copy-start | bytes 12292
  226.8 78.7 %all-to-all-start = ((bf16[16,128,768]{2,1,0:T(8,128)(2,1)}), bf16[16,128,768]{2,1,0:T(8,128)(2,1)}, u32[]{:S(2)}, u32[]{:S(2)}) async-start(bf16[16,128,768]{2,1,0:T(8,128)(2,1)} %bitcast.427), calls=%async_computation | async-start | bytes 6291456 | tf_op jit(solution)/shard_map/all_to_all | solution.py:47
  238.8 363.1 %copy-start.45 = (f32[1024,16]{0,1:T(8,128)}, f32[1024,16]{0,1:T(8,128)S(1)}, u32[]{:S(2)}) copy-start(f32[1024,16]{0,1:T(8,128)S(1)} %get-tuple-element.456) | copy-start | bytes 196612
  238.9 363.1 %copy-start.61 = (f32[1024]{0:T(1024)}, f32[1024]{0:T(1024)S(1)}, u32[]{:S(2)}) copy-start(f32[1024]{0:T(1024)S(1)} %get-tuple-element.455) | copy-start | bytes 12292
  238.9 363.1 %copy-start.67 = (f32[1024]{0:T(1024)}, f32[1024]{0:T(1024)S(1)}, u32[]{:S(2)}) copy-start(f32[1024]{0:T(1024)S(1)} %fusion.138) | copy-start | bytes 12292
  239.0 369.3 %copy-start.65 = (f32[1024]{0:T(1024)}, f32[1024]{0:T(1024)S(1)}, u32[]{:S(2)}) copy-start(f32[1024]{0:T(1024)S(1)} %fusion.133) | copy-start | bytes 12292
  305.5 76.1 %all-to-all-start.2 = ((bf16[16,128,768]{2,1,0:T(8,128)(2,1)}), bf16[16,128,768]{2,1,0:T(8,128)(2,1)}, u32[]{:S(2)}, u32[]{:S(2)}) async-start(bf16[16,128,768]{2,1,0:T(8,128)(2,1)} %bitcast.428), calls=%async_computation.2 | async-start | bytes 6291456 | tf_op jit(solution)/shard_map/all_to_all | solution.py:47
  519.0 75.1 %all-to-all-start.3 = ((bf16[16,128,768]{2,1,0:T(8,128)(2,1)}), bf16[16,128,768]{2,1,0:T(8,128)(2,1)}, u32[]{:S(2)}, u32[]{:S(2)}) async-start(bf16[16,128,768]{2,1,0:T(8,128)(2,1)} %get-tuple-element.314), calls=%async_computation.3 | async-start | bytes 6291456 | tf_op jit(solution)/shard_map/all_to_all | solution.py:53
  524.4 503.2 %all-reduce.10.cloned.1.call-start = ((), (), s32[]{:S(2)}) async-start(), calls=%async_computation.5 | async-start | bytes 6291456 | tf_op jit(solution)/shard_map/psum | solution.py:42
  534.8 67.2 %copy-start.69 = (f32[1024]{0:T(1024)}, f32[1024]{0:T(1024)S(1)}, u32[]{:S(2)}) copy-start(f32[1024]{0:T(1024)S(1)} %fusion.96) | copy-start | bytes 12292
  641.5 56.4 %copy-start.8 = (pred[512,1024]{1,0:T(8,128)(4,1)}, pred[512,1024]{1,0:T(8,128)(4,1)S(1)}, u32[]{:S(2)}) copy-start(pred[512,1024]{1,0:T(8,128)(4,1)S(1)} %get-tuple-element.841) | copy-start | bytes 1572868 | tf_op jit(solution)/shard_map/while
  641.5 56.4 %copy-start.9 = (pred[512,1024]{1,0:T(8,128)(4,1)}, pred[512,1024]{1,0:T(8,128)(4,1)S(1)}, u32[]{:S(2)}) copy-start(pred[512,1024]{1,0:T(8,128)(4,1)S(1)} %get-tuple-element.840) | copy-start | bytes 1572868 | tf_op jit(solution)/shard_map/while
  641.5 56.4 %copy-start.10 = (pred[512,1024]{1,0:T(8,128)(4,1)}, pred[512,1024]{1,0:T(8,128)(4,1)S(1)}, u32[]{:S(2)}) copy-start(pred[512,1024]{1,0:T(8,128)(4,1)S(1)} %get-tuple-element.839) | copy-start | bytes 1572868 | tf_op jit(solution)/shard_map/while
  641.5 56.4 %copy-start.11 = (pred[512,1024]{1,0:T(8,128)(4,1)}, pred[512,1024]{1,0:T(8,128)(4,1)S(1)}, u32[]{:S(2)}) copy-start(pred[512,1024]{1,0:T(8,128)(4,1)S(1)} %get-tuple-element.838) | copy-start | bytes 1572868 | tf_op jit(solution)/shard_map/while
  641.5 56.4 %copy-start.12 = (pred[512,1024]{1,0:T(8,128)(4,1)}, pred[512,1024]{1,0:T(8,128)(4,1)S(1)}, u32[]{:S(2)}) copy-start(pred[512,1024]{1,0:T(8,128)(4,1)S(1)} %get-tuple-element.837) | copy-start | bytes 1572868 | tf_op jit(solution)/shard_map/while
  641.5 56.4 %copy-start.13 = (pred[512,1024]{1,0:T(8,128)(4,1)}, pred[512,1024]{1,0:T(8,128)(4,1)S(1)}, u32[]{:S(2)}) copy-start(pred[512,1024]{1,0:T(8,128)(4,1)S(1)} %get-tuple-element.836) | copy-start | bytes 1572868 | tf_op jit(solution)/shard_map/while
  641.5 56.4 %copy-start.14 = (pred[512,1024]{1,0:T(8,128)(4,1)}, pred[512,1024]{1,0:T(8,128)(4,1)S(1)}, u32[]{:S(2)}) copy-start(pred[512,1024]{1,0:T(8,128)(4,1)S(1)} %get-tuple-element.835) | copy-start | bytes 1572868 | tf_op jit(solution)/shard_map/while
  641.6 56.4 %copy-start.15 = (pred[512,1024]{1,0:T(8,128)(4,1)}, pred[512,1024]{1,0:T(8,128)(4,1)S(1)}, u32[]{:S(2)}) copy-start(pred[512,1024]{1,0:T(8,128)(4,1)S(1)} %get-tuple-element.898) | copy-start | bytes 1572868 | tf_op jit(solution)/shard_map/while
  641.6 56.4 %copy-start.17 = (pred[512,1024]{1,0:T(8,128)(4,1)}, pred[512,1024]{1,0:T(8,128)(4,1)S(1)}, u32[]{:S(2)}) copy-start(pred[512,1024]{1,0:T(8,128)(4,1)S(1)} %get-tuple-element.896) | copy-start | bytes 1572868 | tf_op jit(solution)/shard_map/while
  641.6 56.4 %copy-start.19 = (pred[512,1024]{1,0:T(8,128)(4,1)}, pred[512,1024]{1,0:T(8,128)(4,1)S(1)}, u32[]{:S(2)}) copy-start(pred[512,1024]{1,0:T(8,128)(4,1)S(1)} %get-tuple-element.894) | copy-start | bytes 1572868 | tf_op jit(solution)/shard_map/while
  641.6 56.4 %copy-start.21 = (pred[512,1024]{1,0:T(8,128)(4,1)}, pred[512,1024]{1,0:T(8,128)(4,1)S(1)}, u32[]{:S(2)}) copy-start(pred[512,1024]{1,0:T(8,128)(4,1)S(1)} %get-tuple-element.892) | copy-start | bytes 1572868 | tf_op jit(solution)/shard_map/while
  641.6 56.4 %copy-start.23 = (pred[512,1024]{1,0:T(8,128)(4,1)}, pred[512,1024]{1,0:T(8,128)(4,1)S(1)}, u32[]{:S(2)}) copy-start(pred[512,1024]{1,0:T(8,128)(4,1)S(1)} %get-tuple-element.890) | copy-start | bytes 1572868 | tf_op jit(solution)/shard_map/while
  825.5 56.4 %copy-start.8 = (pred[512,1024]{1,0:T(8,128)(4,1)}, pred[512,1024]{1,0:T(8,128)(4,1)S(1)}, u32[]{:S(2)}) copy-start(pred[512,1024]{1,0:T(8,128)(4,1)S(1)} %get-tuple-element.841) | copy-start | bytes 1572868 | tf_op jit(solution)/shard_map/while
  825.5 56.4 %copy-start.9 = (pred[512,1024]{1,0:T(8,128)(4,1)}, pred[512,1024]{1,0:T(8,128)(4,1)S(1)}, u32[]{:S(2)}) copy-start(pred[512,1024]{1,0:T(8,128)(4,1)S(1)} %get-tuple-element.840) | copy-start | bytes 1572868 | tf_op jit(solution)/shard_map/while
  825.5 56.4 %copy-start.10 = (pred[512,1024]{1,0:T(8,128)(4,1)}, pred[512,1024]{1,0:T(8,128)(4,1)S(1)}, u32[]{:S(2)}) copy-start(pred[512,1024]{1,0:T(8,128)(4,1)S(1)} %get-tuple-element.839) | copy-start | bytes 1572868 | tf_op jit(solution)/shard_map/while
  825.6 56.4 %copy-start.11 = (pred[512,1024]{1,0:T(8,128)(4,1)}, pred[512,1024]{1,0:T(8,128)(4,1)S(1)}, u32[]{:S(2)}) copy-start(pred[512,1024]{1,0:T(8,128)(4,1)S(1)} %get-tuple-element.838) | copy-start | bytes 1572868 | tf_op jit(solution)/shard_map/while
  825.6 56.4 %copy-start.12 = (pred[512,1024]{1,0:T(8,128)(4,1)}, pred[512,1024]{1,0:T(8,128)(4,1)S(1)}, u32[]{:S(2)}) copy-start(pred[512,1024]{1,0:T(8,128)(4,1)S(1)} %get-tuple-element.837) | copy-start | bytes 1572868 | tf_op jit(solution)/shard_map/while
  825.6 56.4 %copy-start.13 = (pred[512,1024]{1,0:T(8,128)(4,1)}, pred[512,1024]{1,0:T(8,128)(4,1)S(1)}, u32[]{:S(2)}) copy-start(pred[512,1024]{1,0:T(8,128)(4,1)S(1)} %get-tuple-element.836) | copy-start | bytes 1572868 | tf_op jit(solution)/shard_map/while
  825.6 56.4 %copy-start.14 = (pred[512,1024]{1,0:T(8,128)(4,1)}, pred[512,1024]{1,0:T(8,128)(4,1)S(1)}, u32[]{:S(2)}) copy-start(pred[512,1024]{1,0:T(8,128)(4,1)S(1)} %get-tuple-element.835) | copy-start | bytes 1572868 | tf_op jit(solution)/shard_map/while
  994.0 209.4 %all-reduce.12.cloned.1.call-start = ((), (), s32[]{:S(2)}) async-start(), calls=%async_computation.6 | async-start | bytes 9437184 | tf_op jit(solution)/shard_map/psum | solution.py:256
  (93 other events, 1173.5 us)
Sparse Core Ops, SparseCore 0:
  189.3 24.5 all-reduce.7
  994.1 22.2 all-reduce.9
  1022.7 180.6 all-reduce.11
where the time goes:
time: 1230 us; the launch traced here: 1220 us
  matrix products  378 us (31%)
  waiting for transfers between devices  284 us (23%)
  other arithmetic  227 us (18%)
  blocking collectives  180 us (15%)
  local copies, waits for them, and re-layouts  104 us (8%)
  starting transfers between devices  18.9 us (2%)
  between operations  14.5 us (1%)
    dot_general x4, matrix products, score_block(): jnp.einsum('qhd,khd->hqk', query_block, keys_all, preferred_element_type=...  215 us
    reduce_sum x4, other arithmetic, table_from_grads(): columns.append(jnp.sum(masked, axis=(1, 2)))  120 us
    all_to_all x2, waiting for transfers between devices, to_owners(): lax.all_to_all(grouped, 'dp', split_axis=0, concat_axis=0, tiled=True)  106 us
    psum x1, waiting for transfers between devices, per_device(): lax.psum((grad_gain_attn, grad_w_qkv, grad_w_attn_out, grad_table.T, grad...  98.6 us
    all_to_all x1, blocking collectives, to_senders(): lax.all_to_all(summed.astype(jnp.bfloat16), 'dp', split_axis=0, concat_ax...  75.6 us
    psum x1, blocking collectives, per_device(): lax.psum((grad_gain_attn, grad_w_qkv, grad_w_attn_out, grad_table.T, grad...  68.8 us
    all_to_all x1, waiting for transfers between devices, to_senders(): lax.all_to_all(summed.astype(jnp.bfloat16), 'dp', split_axis=0, concat_ax...  59.4 us
    eq x4, other arithmetic, bias_from_table(): bias_sum = bias_sum + jnp.where(bucket[None] == bucket_number, column, 0.0)  53.9 us
  transfers between devices with their start and end apart: 6, of which 5 were waited for; matrix products, arithmetic and copies ran while one was open for 7% of the time, Pallas kernels for 0%

commit v1 on v0

v1 whole, which is shorter than its diff:
```python
import jax
import jax.numpy as jnp
from jax import lax
from jax.experimental import pallas as pl
from jax.experimental.pallas import tpu as pltpu
from jax.sharding import PartitionSpec as P

epsilon = 1e-06
highest = lax.Precision.HIGHEST
bucket_edges = (8, 12, 16, 23, 32, 46, 64, 91)


def bucket_ids(row_positions, col_positions, half_count):
    offset = col_positions[None, :] - row_positions[:, None]
    distance = jnp.abs(offset)
    far_part = jnp.zeros_like(distance)
    for edge_value in bucket_edges:
        far_part = far_part + (distance >= edge_value).astype(jnp.int32)
    near_far = jnp.where(distance < 8, distance, 7 + far_part)
    return near_far + half_count * (offset > 0).astype(jnp.int32)


NEAR = 128
ROWS = 256
SPAN = ROWS + 2 * NEAR


def near_buckets(bucket_count):
    zero = jnp.zeros((1,), jnp.int32)
    relative = jnp.arange(SPAN, dtype=jnp.int32) - NEAR
    return bucket_ids(zero, relative, bucket_count // 2)[0]


def skew(values, right):
    rows = lax.broadcasted_iota(jnp.int32, values.shape, 0)
    width = values.shape[1]
    step = 1
    while step < values.shape[0]:
        rolled = pltpu.roll(values, step if right else width - step, 1)
        values = jnp.where((rows & step) != 0, rolled, values)
        step *= 2
    return values


def fill_strip(strip, vec_ref, length):
    left = length - ROWS - NEAR
    for head in range(2):
        row = vec_ref[0, head : head + 1, :]
        low = row[:, :1]
        high = row[:, SPAN - 1 :]
        spread = skew(jnp.broadcast_to(row, (ROWS, SPAN)), True)
        lanes = lax.broadcasted_iota(jnp.int32, (ROWS, SPAN), 1)
        rows = lax.broadcasted_iota(jnp.int32, (ROWS, SPAN), 0)
        strip[head, :, left : left + SPAN] = jnp.where(lanes < rows, low, spread)
        strip[head, :, :left] = jnp.broadcast_to(low, (ROWS, left))
        rest = strip.shape[2] - left - SPAN
        strip[head, :, left + SPAN :] = jnp.broadcast_to(high, (ROWS, rest))


def head_lanes(values, head):
    lanes = lax.broadcasted_iota(jnp.int32, values.shape, 1)
    keep = (lanes < 64) if head == 0 else (lanes >= 64)
    return jnp.where(keep, values, jnp.zeros_like(values))


def dot_nt(left, right):
    return lax.dot_general(left, right, (((1,), (1,)), ((), ())), preferred_element_type=jnp.float32)


def dot_tn(left, right):
    return lax.dot_general(left, right, (((0,), (0,)), ((), ())), preferred_element_type=jnp.float32)


def dot_nn(left, right):
    return jnp.dot(left, right, preferred_element_type=jnp.float32)


def forward_kernel(q_ref, k_ref, v_ref, seg_col, seg_row, vec_ref, out_ref, lse_ref, strip):
    length = k_ref.shape[0]
    block = pl.program_id(1)

    @pl.when(block == 0)
    def _():
        fill_strip(strip, vec_ref, length)

    start = pl.multiple_of(length - ROWS - block * ROWS, ROWS)
    same_doc = seg_col[...] == seg_row[...]
    outs = []
    norms = []
    for head in range(2):
        scores = dot_nt(head_lanes(q_ref[...], head), k_ref[...]) * 0.125
        scores = scores + strip[head, :, pl.ds(start, length)]
        scores = jnp.where(same_doc, scores, -1e30)
        peak = jnp.max(scores, axis=1, keepdims=True)
        shifted = jnp.exp(scores - peak)
        total = jnp.sum(shifted, axis=1, keepdims=True)
        weights = (shifted * (1.0 / total)).astype(jnp.bfloat16)
        outs.append(dot_nn(weights, v_ref[...]))
        norms.append(peak + jnp.log(total))
    lanes = lax.broadcasted_iota(jnp.int32, out_ref.shape, 1)
    out_ref[...] = jnp.where(lanes < 64, outs[0], outs[1]).astype(jnp.bfloat16)
    lse_ref[...] = jnp.where(lanes < 64, norms[0], norms[1])


def backward_kernel(
    q_ref, k_ref, v_ref, g_ref, seg_col, seg_row, vec_ref, lse_ref,
    dq_ref, dk_ref, dv_ref, diag_ref, far_ref, strip, sums, dk_sum, dv_sum,
):
    length = k_ref.shape[0]
    block = pl.program_id(1)
    left = length - ROWS - NEAR

    @pl.when(block == 0)
    def _():
        fill_strip(strip, vec_ref, length)
        sums[...] = jnp.zeros_like(sums)
        dk_sum[...] = jnp.zeros_like(dk_sum)
        dv_sum[...] = jnp.zeros_like(dv_sum)

    start = pl.multiple_of(length - ROWS - block * ROWS, ROWS)
    same_doc = seg_col[...] == seg_row[...]
    queries_grad = []
    for head in range(2):
        query = head_lanes(q_ref[...], head)
        out_grad = head_lanes(g_ref[...], head)
        scores = dot_nt(query, k_ref[...]) * 0.125
        scores = scores + strip[head, :, pl.ds(start, length)]
        norm = lse_ref[:, 64 * head : 64 * head + 1]
        probs = jnp.where(same_doc, jnp.exp(scores - norm), 0.0)
        grad_probs = dot_nt(out_grad, v_ref[...])
        row_dot = jnp.sum(probs * grad_probs, axis=1, keepdims=True)
        grad_scores = probs * (grad_probs - row_dot)
        sums[head, :, pl.ds(start, length)] += grad_scores
        low_scores = grad_scores.astype(jnp.bfloat16)
        queries_grad.append(dot_nn(low_scores, k_ref[...]))
        dk_sum[...] += dot_tn(low_scores, query)
        dv_sum[...] += dot_tn(probs.astype(jnp.bfloat16), out_grad)
    lanes = lax.broadcasted_iota(jnp.int32, dq_ref.shape, 1)
    joined = jnp.where(lanes < 64, queries_grad[0], queries_grad[1]) * 0.125
    dq_ref[...] = joined.astype(jnp.bfloat16)

    @pl.when(block == pl.num_programs(1) - 1)
    def _():
        dk_ref[...] = (dk_sum[...] * 0.125).astype(jnp.bfloat16)
        dv_ref[...] = dv_sum[...].astype(jnp.bfloat16)
        for head in range(2):
            near = sums[head, :, left : left + SPAN]
            lanes = lax.broadcasted_iota(jnp.int32, near.shape, 1)
            rows = lax.broadcasted_iota(jnp.int32, near.shape, 0)
            relative = lanes - rows - NEAR
            low = jnp.sum(jnp.where(relative <= -NEAR, near, 0.0), axis=0, keepdims=True)
            high = jnp.sum(jnp.where(relative >= NEAR, near, 0.0), axis=0, keepdims=True)
            inside = jnp.where(jnp.abs(relative) < NEAR, near, 0.0)
            diag_ref[0, head : head + 1, :] = jnp.sum(skew(inside, False), axis=0, keepdims=True)
            low_total = jnp.sum(low) + jnp.sum(sums[head, :, :left])
            high_total = jnp.sum(high) + jnp.sum(sums[head, :, left + SPAN :])
            side = lax.broadcasted_iota(jnp.int32, (1, 128), 1)
            far_ref[0, head : head + 1, :] = jnp.where(side < 64, low_total, high_total)


def attention_specs(length, pairs):
    whole = lambda part: pl.BlockSpec((length, 128), lambda p, b: (0, part * pairs + p))
    rows = pl.BlockSpec((ROWS, 128), lambda p, b: (b, p))
    seg_col = pl.BlockSpec((ROWS, 1), lambda p, b: (b, 0))
    seg_row = pl.BlockSpec((1, length), lambda p, b: (0, 0))
    vec = pl.BlockSpec((1, 2, SPAN), lambda p, b: (p, 0, 0))
    return whole, rows, seg_col, seg_row, vec


def attention_forward(packed, segment_row, bias_vec):
    length = packed.shape[0]
    pairs = packed.shape[1] // (3 * 128)
    whole, rows, seg_col, seg_row, vec = attention_specs(length, pairs)
    return pl.pallas_call(
        forward_kernel,
        grid=(pairs, length // ROWS),
        in_specs=[rows, whole(1), whole(2), seg_col, seg_row, vec],
        out_specs=[rows, rows],
        out_shape=[
            jax.ShapeDtypeStruct((length, pairs * 128), jnp.bfloat16),
            jax.ShapeDtypeStruct((length, pairs * 128), jnp.float32),
        ],
        scratch_shapes=[pltpu.VMEM((2, ROWS, 2 * length - ROWS), jnp.float32)],
        compiler_params=pltpu.CompilerParams(vmem_limit_bytes=40 * 1024 * 1024),
        name="attention_forward",
    )(packed, packed, packed, segment_row[:, None], segment_row[None, :], bias_vec)


def attention_backward(packed, out_grad, segment_row, bias_vec, log_norm):
    length = packed.shape[0]
    pairs = packed.shape[1] // (3 * 128)
    whole, rows, seg_col, seg_row, vec = attention_specs(length, pairs)
    low = jax.ShapeDtypeStruct((length, pairs * 128), jnp.bfloat16)
    return pl.pallas_call(
        backward_kernel,
        grid=(pairs, length // ROWS),
        in_specs=[rows, whole(1), whole(2), rows, seg_col, seg_row, vec, rows],
        out_specs=[
            rows,
            whole(0),
            whole(0),
            vec,
            pl.BlockSpec((1, 2, 128), lambda p, b: (p, 0, 0)),
        ],
        out_shape=[
            low,
            low,
            low,
            jax.ShapeDtypeStruct((pairs, 2, SPAN), jnp.float32),
            jax.ShapeDtypeStruct((pairs, 2, 128), jnp.float32),
        ],
        scratch_shapes=[
            pltpu.VMEM((2, ROWS, 2 * length - ROWS), jnp.float32),
            pltpu.VMEM((2, ROWS, 2 * length - ROWS), jnp.float32),
            pltpu.VMEM((length, 128), jnp.float32),
            pltpu.VMEM((length, 128), jnp.float32),
        ],
        compiler_params=pltpu.CompilerParams(vmem_limit_bytes=48 * 1024 * 1024),
        name="attention_backward",
    )(packed, packed, packed, out_grad, segment_row[:, None], segment_row[None, :], bias_vec, log_norm)


def gelu_tanh(inner_act):
    return jax.nn.gelu(inner_act, approximate=True)


def swap(values):
    return lax.ppermute(values, "tensor", [(0, 1), (1, 0)])


def heads_total(partial_sum):
    return partial_sum + swap(partial_sum)


def exchange(rows, model_width):
    grouped = rows.reshape(lax.axis_size("dp"), -1, model_width)
    return lax.all_to_all(grouped, "dp", split_axis=0, concat_axis=0, tiled=True)


def to_owners(rows, model_width):
    arrived = exchange(rows, model_width)
    return jnp.concatenate([arrived, swap(arrived)], axis=0)


def to_senders(partial_rows, model_width):
    kept, given = jnp.split(partial_rows.reshape(2, -1, model_width), 2, axis=0)
    summed = kept + swap(given.astype(jnp.bfloat16)).astype(jnp.float32)
    arrived = exchange(summed.astype(jnp.bfloat16), model_width).reshape(-1, model_width)
    return jnp.concatenate([arrived, swap(arrived)], axis=0)


def per_device(
    tokens,
    segments,
    gain_attn,
    w_qkv,
    w_attn_out,
    bias_table,
    gain_ffn,
    router,
    expert_in,
    expert_out,
    expert_ids,
    cotangent,
):
    length, model_width = tokens.shape
    head_cols = w_qkv.shape[2]
    heads_here = bias_table.shape[1]
    head_size = head_cols // heads_here
    experts_all = router.shape[1]
    experts_here = expert_in.shape[0]
    capacity = max(2, 2 * length // experts_all)
    half = capacity // 2
    segment_row = segments[0]
    bucket_count = bias_table.shape[0]
    near_hot = (
        near_buckets(bucket_count)[:, None] == jnp.arange(bucket_count, dtype=jnp.int32)[None, :]
    ).astype(jnp.float32)
    bias_vec = jnp.sum(near_hot[None] * bias_table.T[:, None, :], axis=2)
    bias_vec = bias_vec.reshape(heads_here // 2, 2, SPAN)
    inputs32 = tokens.astype(jnp.float32)
    scale_one = lax.rsqrt(jnp.mean(inputs32 * inputs32, axis=1, keepdims=True) + epsilon)
    normed_one = inputs32 * scale_one
    normed = (normed_one * gain_attn).astype(jnp.bfloat16)
    w_flat = w_qkv.reshape(model_width, 3 * head_cols)
    packed = jnp.dot(normed, w_flat, preferred_element_type=jnp.float32).astype(jnp.bfloat16)
    mixed_heads, log_norm = attention_forward(packed, segment_row, bias_vec)
    attn_part = jnp.dot(mixed_heads, w_attn_out, preferred_element_type=jnp.float32)
    hidden = inputs32 + heads_total(attn_part)
    scale_two = lax.rsqrt(jnp.mean(hidden * hidden, axis=1, keepdims=True) + epsilon)
    normed_two = hidden * scale_two
    ffn_in = normed_two * gain_ffn
    router_logits = jnp.dot(ffn_in, router, precision=highest)
    logit_peak = jnp.max(router_logits, axis=1, keepdims=True)
    router_exp = jnp.exp(router_logits - logit_peak)
    router_probs = router_exp / jnp.sum(router_exp, axis=1, keepdims=True)
    chosen = expert_ids[:, 0]
    one_hot_int = (chosen[:, None] == jnp.arange(experts_all, dtype=jnp.int32)[None, :]).astype(
        jnp.int32
    )
    one_hot_float = one_hot_int.astype(jnp.float32)
    gate_prob = jnp.sum(router_probs * one_hot_float, axis=1)
    earlier = jnp.arange(length)[None, :] < jnp.arange(length)[:, None]
    ranks = jnp.dot(
        earlier.astype(jnp.bfloat16),
        one_hot_float.astype(jnp.bfloat16),
        preferred_element_type=jnp.float32,
    )
    slot_ids = jnp.sum(ranks * one_hot_float, axis=1).astype(jnp.int32)
    side = (slot_ids >= half).astype(jnp.int32)
    other_side = (side != lax.axis_index("tensor")).astype(jnp.int32)
    target_rows = chosen * half + slot_ids - side * half + other_side * (experts_all * half)
    own_slots = jnp.arange(experts_all * half, dtype=jnp.int32)
    place = (own_slots[:, None] == target_rows[None, :]).astype(jnp.bfloat16)
    all_slots = jnp.arange(2 * experts_all * half, dtype=jnp.int32)
    pick = (target_rows[:, None] == all_slots[None, :]).astype(jnp.bfloat16)
    send_rows = jnp.dot(place, ffn_in.astype(jnp.bfloat16), preferred_element_type=jnp.float32)
    expert_rows = to_owners(send_rows.astype(jnp.bfloat16), model_width).reshape(
        -1, experts_here, half, model_width
    )
    upstream = cotangent.astype(jnp.float32)
    back_rows = (gate_prob[:, None] * upstream).astype(jnp.bfloat16)
    back_sent = jnp.dot(place, back_rows, preferred_element_type=jnp.float32)
    expert_grads = to_owners(back_sent.astype(jnp.bfloat16), model_width).reshape(
        -1, experts_here, half, model_width
    )
    inner_act = jnp.einsum(
        "secd,edf->secf", expert_rows, expert_in, preferred_element_type=jnp.float32
    )
    activated, gelu_back = jax.vjp(gelu_tanh, inner_act)
    act_low = activated.astype(jnp.bfloat16)
    expert_part = jnp.einsum(
        "secf,efd->secd", act_low, expert_out, preferred_element_type=jnp.float32
    )
    returned = to_senders(expert_part, model_width)
    picked = jnp.dot(pick, returned, preferred_element_type=jnp.float32)
    output = (hidden + gate_prob[:, None] * picked).astype(jnp.bfloat16)
    grad_gate = jnp.sum(upstream * picked, axis=1)
    grad_act = jnp.einsum(
        "secd,efd->secf", expert_grads, expert_out, preferred_element_type=jnp.float32
    )
    grad_inner = gelu_back(grad_act)[0].astype(jnp.bfloat16)
    grad_expert_out = jnp.einsum(
        "secf,secd->efd", act_low, expert_grads, preferred_element_type=jnp.float32
    )
    grad_expert_in = jnp.einsum(
        "secd,secf->edf", expert_rows, grad_inner, preferred_element_type=jnp.float32
    )
    grad_rows = jnp.einsum(
        "secf,edf->secd", grad_inner, expert_in, preferred_element_type=jnp.float32
    )
    grad_sent = jnp.dot(
        pick, to_senders(grad_rows, model_width), preferred_element_type=jnp.float32
    )
    grad_logits = router_probs * (one_hot_float - gate_prob[:, None]) * grad_gate[:, None]
    grad_router = jnp.dot(ffn_in.T, grad_logits, precision=highest)
    grad_ffn_in = grad_sent + jnp.dot(grad_logits, router.T, precision=highest)
    grad_gain_ffn = jnp.sum(grad_ffn_in * normed_two, axis=0)
    grad_norm_two = grad_ffn_in * gain_ffn
    grad_hidden = upstream + scale_two * (
        grad_norm_two - normed_two * jnp.mean(grad_norm_two * normed_two, axis=1, keepdims=True)
    )
    grad_attn = grad_hidden.astype(jnp.bfloat16)
    grad_w_attn_out = jnp.dot(mixed_heads.T, grad_attn, preferred_element_type=jnp.float32)
    grad_mixed = jnp.dot(grad_attn, w_attn_out.T, preferred_element_type=jnp.float32).astype(
        jnp.bfloat16
    )
    early = lax.psum(
        (grad_w_attn_out.astype(jnp.bfloat16), grad_gain_ffn, grad_router), "dp"
    )
    grad_queries, grad_keys, grad_values, diagonals, far = attention_backward(
        packed, grad_mixed, segment_row, bias_vec, log_norm
    )
    grad_table = jnp.sum(diagonals.reshape(heads_here, SPAN)[:, :, None] * near_hot[None], axis=1)
    far = far.reshape(heads_here, 128)
    half_count = bucket_count // 2
    bucket_row = jnp.arange(bucket_count, dtype=jnp.int32)[None, :]
    grad_table = grad_table + jnp.where(bucket_row == half_count - 1, far[:, :1], 0.0)
    grad_table = grad_table + jnp.where(bucket_row == bucket_count - 1, far[:, 127:], 0.0)
    grad_packed = jnp.concatenate([grad_queries, grad_keys, grad_values], axis=1)
    grad_packed, early = lax.optimization_barrier((grad_packed, early))
    grad_w_qkv = jnp.dot(normed.T, grad_packed, preferred_element_type=jnp.float32).reshape(
        model_width, 3, head_cols
    )
    grad_normed = heads_total(jnp.dot(grad_packed, w_flat.T, preferred_element_type=jnp.float32))
    grad_gain_attn = jnp.sum(grad_normed * normed_one, axis=0)
    grad_norm_one = grad_normed * gain_attn
    grad_tokens = grad_hidden + scale_one * (
        grad_norm_one - normed_one * jnp.mean(grad_norm_one * normed_one, axis=1, keepdims=True)
    )
    total_w_qkv = lax.psum(grad_w_qkv.astype(jnp.bfloat16), "dp")
    total_gain, total_table = lax.psum((grad_gain_attn, grad_table.T), "dp")
    return (
        output,
        grad_tokens,
        total_gain,
        total_w_qkv.astype(jnp.float32),
        early[0].astype(jnp.float32),
        total_table,
        early[1],
        early[2],
        grad_expert_in,
        grad_expert_out,
    )


def solution(mesh):
    return jax.shard_map(
        per_device,
        mesh=mesh,
        in_specs=(
            P("dp", None),
            P("dp", None),
            P(),
            P(None, None, "tensor"),
            P("tensor", None),
            P(None, "tensor"),
            P(),
            P(),
            P("dp", None, "tensor"),
            P("dp", "tensor", None),
            P("dp", None),
            P("dp", None),
        ),
        out_specs=(
            P("dp", None),
            P("dp", None),
            P(),
            P(None, None, "tensor"),
            P("tensor", None),
            P(None, "tensor"),
            P(),
            P(),
            P("dp", None, "tensor"),
            P("dp", "tensor", None),
        ),
        check_vma=False,
    )
```

time: 1230 us -> 648 us (0.53)
  the two profiles are of different devices: /device:TPU:12 before, /device:TPU:0 now
where the time goes in v1:
time: 648 us; the launch traced here: 639 us
  waiting for transfers between devices  220 us (34%)
  blocking collectives  120 us (19%)
  matrix products  114 us (18%)
  Pallas kernels  66.9 us (10%)
  local copies, waits for them, and re-layouts  39.8 us (6%)
  starting transfers between devices  33.9 us (5%)
  other arithmetic  28.7 us (4%)
  between operations  15.4 us (2%)
    all_to_all x4, waiting for transfers between devices, exchange(): lax.all_to_all(grouped, 'dp', split_axis=0, concat_axis=0, tiled=True)  107 us
    psum x1, waiting for transfers between devices, per_device(): total_w_qkv = lax.psum(grad_w_qkv.astype(jnp.bfloat16), 'dp')  103 us
    psum x1, blocking collectives, per_device(): lax.psum((grad_w_attn_out.astype(jnp.bfloat16), grad_gain_ffn, grad_route...  78.7 us
    pallas_call x1, Pallas kernels, attention_backward(): pl.pallas_call(backward_kernel, grid=(pairs, length // ROWS), in_specs=[r...  41.8 us
    psum x1, blocking collectives, per_device(): total_gain, total_table = lax.psum((grad_gain_attn, grad_table.T), 'dp')  41 us
    all_to_all x4, starting transfers between devices, exchange(): lax.all_to_all(grouped, 'dp', split_axis=0, concat_axis=0, tiled=True)  32.6 us
    unnamed x130, local copies, waits for them, and re-layouts  32.3 us
    pallas_call x1, Pallas kernels, attention_forward(): pl.pallas_call(forward_kernel, grid=(pairs, length // ROWS), in_specs=[ro...  25.1 us
  transfers between devices with their start and end apart: 14, of which 8 were waited for; matrix products, arithmetic and copies ran while one was open for 14% of the time, Pallas kernels for 7%

profile of v1, /device:TPU:0, one launch (start us, length us, event | category | flops | bytes accessed | tf_op | source)
XLA Modules:
  0.0 638.8 jit_solution(17124939774624240341)
XLA Ops:
  14.1 3.9 copy.49
  17.9 4.4 convolution_convert_fusion.q_ref.k_ref.v_ref
  22.4 25.1 %attention_forward.1 = (bf16[1024,384]{1,0:T(8,128)(2,1)S(1)}, f32[1024,384]{1,0:T(8,128)S(1)}) custom-call(bf16[1024,1152]{1,0:T(8,128)(2,1)S(1)} %convolution_convert_fusion.q_ref.k_ref.v_ref, bf16[1024,1152]{1,0:T(8,128)(2,1)S(1)} %convolution_convert_fusion.q_ref.k_ref.v_ref, bf16[1024,1152]{1,0:T(8,128)(2,1)S(1)} %convolution_convert_fusion.q_ref.k_ref.v_ref, ...), custom_call_target="tpu_custom_call" | custom-call | tf_op jit(solution)/shard_map/attention_forward/pallas_call | solution.py:174
  52.6 4.5 collective-permute-done
  57.1 4.2 multiply_reduce_fusion.2
  66.2 8.5 %all-to-all-start = ((bf16[16,64,768]{2,1,0:T(8,128)(2,1)}), bf16[16,64,768]{2,1,0:T(8,128)(2,1)}, u32[]{:S(2)}, u32[]{:S(2)}) async-start(bf16[16,64,768]{2,1,0:T(8,128)(2,1)} %bitcast.138), calls=%async_computation | async-start | bytes 3145728 | tf_op jit(solution)/shard_map/all_to_all | solution.py:237
  77.3 4.0 fusion.131
  86.4 22.7 %all-to-all-done = bf16[16,64,768]{2,1,0:T(8,128)(2,1)} async-done(((bf16[16,64,768]{2,1,0:T(8,128)(2,1)}), bf16[16,64,768]{2,1,0:T(8,128)(2,1)}, u32[]{:S(2)}, u32[]{:S(2)}) %all-to-all-start) | async-done | bytes 1572896 | tf_op jit(solution)/shard_map/all_to_all | solution.py:237
  109.0 8.1 %all-to-all-start.2 = ((bf16[16,64,768]{2,1,0:T(8,128)(2,1)}), bf16[16,64,768]{2,1,0:T(8,128)(2,1)}, u32[]{:S(2)}, u32[]{:S(2)}) async-start(bf16[16,64,768]{2,1,0:T(8,128)(2,1)} %bitcast.137), calls=%async_computation.2 | async-start | bytes 3145728 | tf_op jit(solution)/shard_map/all_to_all | solution.py:237
  117.2 33.4 %all-to-all-done.2 = bf16[16,64,768]{2,1,0:T(8,128)(2,1)} async-done(((bf16[16,64,768]{2,1,0:T(8,128)(2,1)}), bf16[16,64,768]{2,1,0:T(8,128)(2,1)}, u32[]{:S(2)}, u32[]{:S(2)}) %all-to-all-start.2) | async-done | bytes 1572896 | tf_op jit(solution)/shard_map/all_to_all | solution.py:237
  155.2 7.8 %fusion.66 = f32[32,64,1536]{2,1,0:T(8,128)} fusion(bf16[32,64,768]{2,1,0:T(8,128)(2,1)S(1)} %constant_dynamic-update-slice_fusion, bf16[1,768,1536]{2,1,0:T(8,128)(2,1)S(1)} %copy-done), kind=kOutput, calls=%fused_computation.84 | convolution fusion | flops 4831838208 | bytes 18087936 | tf_op jit(solution)/shard_map/secd,edf->secf/dot_general | solution.py:327
  164.7 16.0 %fusion.6 = bf16[32,1,64,1536]{3,2,0,1:T(8,128)(2,1)S(1)} fusion(f32[32,64,1536]{2,1,0:T(8,128)} %fusion.66, bf16[32,64,768]{2,1,0:T(8,128)(2,1)S(1)} %constant_dynamic-update-slice_fusion.2, bf16[1,1536,768]{2,1,0:T(8,128)(2,1)S(1)} %copy-done.58), kind=kOutput, calls=%fused_computation.8 | convolution fusion | flops 4894752768 | bytes 24379392 | tf_op jit(solution)/shard_map/secd,efd->secf/dot_general | solution.py:339
  180.7 5.2 fusion.60
  191.4 7.7 %all-to-all-start.3 = ((bf16[16,64,768]{2,1,0:T(8,128)(2,1)}), bf16[16,64,768]{2,1,0:T(8,128)(2,1)S(1)}, u32[]{:S(2)}, u32[]{:S(2)}) async-start(bf16[16,64,768]{2,1,0:T(8,128)(2,1)} %bitcast.40), calls=%async_computation.3 | async-start | bytes 3145728 | tf_op jit(solution)/shard_map/all_to_all | solution.py:237
  199.1 11.0 %fusion.57 = f32[32,1,64,768]{3,2,0,1:T(8,128)S(1)} fusion(bf16[1,1536,768]{2,1,0:T(8,128)(2,1)} %param.21, f32[32,64,1536]{2,1,0:T(8,128)} %fusion.66), kind=kOutput, calls=%fused_computation.78 | convolution fusion | flops 4860149760 | bytes 21233664 | tf_op jit(solution)/shard_map/secf,efd->secd/dot_general | solution.py:332
  215.4 17.9 %all-to-all-done.3 = bf16[16,64,768]{2,1,0:T(8,128)(2,1)S(1)} async-done(((bf16[16,64,768]{2,1,0:T(8,128)(2,1)}), bf16[16,64,768]{2,1,0:T(8,128)(2,1)S(1)}, u32[]{:S(2)}, u32[]{:S(2)}) %all-to-all-start.3) | async-done | bytes 1572896 | tf_op jit(solution)/shard_map/all_to_all | solution.py:237
  233.3 8.3 %all-to-all-start.1 = ((bf16[16,64,768]{2,1,0:T(8,128)(2,1)}), bf16[16,64,768]{2,1,0:T(8,128)(2,1)}, u32[]{:S(2)}, u32[]{:S(2)}) async-start(bf16[16,64,768]{2,1,0:T(8,128)(2,1)} %bitcast.24), calls=%async_computation.1 | async-start | bytes 3145728 | tf_op jit(solution)/shard_map/all_to_all | solution.py:237
  242.4 33.1 %all-to-all-done.1 = bf16[16,64,768]{2,1,0:T(8,128)(2,1)} async-done(((bf16[16,64,768]{2,1,0:T(8,128)(2,1)}), bf16[16,64,768]{2,1,0:T(8,128)(2,1)}, u32[]{:S(2)}, u32[]{:S(2)}) %all-to-all-start.1) | async-done | bytes 1572896 | tf_op jit(solution)/shard_map/all_to_all | solution.py:237
  275.5 11.9 %fusion.30 = f32[1,1536,768]{2,1,0:T(8,128)} fusion(bf16[32,64,768]{2,1,0:T(8,128)(2,1)} %copy-done.20, f32[32,64,1536]{2,1,0:T(8,128)} %fusion.66), kind=kOutput, calls=%fused_computation.44 | convolution fusion | flops 4860149760 | bytes 20447232 | tf_op jit(solution)/shard_map/secf,secd->efd/dot_general | solution.py:343
  287.5 5.4 fusion.44
  295.7 6.6 %multiply_reduce_fusion = (f32[768]{0:T(1024)}, f32[1024]{0:T(1024)S(1)}, f32[1024,768]{0,1:T(8,128)S(1)}) fusion(f32[1024,768]{0,1:T(8,128)S(1)} %copy-done.12, f32[1024]{0:T(1024)S(1)} %copy-done.37, f32[768]{0:T(1024)S(1)} %copy-done.43, f32[1024,768]{0,1:T(8,128)S(1)} %fusion.96, bf16[1024,768]{1,0:T(8,128)(2,1)} %collective-permute-done.6, ...), kind=kOutput, calls=%fused_computation.69 | convolution fusion | flops 3235117312 | bytes 12601344 | tf_op jit(solution)/shard_map/dot_general | solution.py:352
  305.4 3.8 convolution_convert_fusion.3
  312.5 41.8 %attention_backward.1 = (bf16[1024,384]{1,0:T(8,128)(2,1)S(1)}, bf16[1024,384]{1,0:T(8,128)(2,1)S(1)}, bf16[1024,384]{1,0:T(8,128)(2,1)S(1)}, f32[3,2,512]{2,1,0:T(2,128)S(1)}, f32[3,2,128]{2,1,0:T(2,128)S(1)}) custom-call(bf16[1024,1152]{1,0:T(8,128)(2,1)} %copy-done.2, bf16[1024,1152]{1,0:T(8,128)(2,1)} %copy-done.2, bf16[1024,1152]{1,0:T(8,128)(2,1)} %copy-done.2, ...), custom_call_target="tpu_custom_call" | custom-call | tf_op jit(solution)/shard_map/attention_backward/pallas_call | solution.py:194
  360.0 78.7 %all-reduce.1 = (f32[768]{0:T(1024)}, f32[768,16]{0,1:T(8,128)}) all-reduce(f32[768]{0:T(1024)S(1)} %copy-done.55, f32[768,16]{0,1:T(8,128)S(1)} %fusion.53), channel_id=1, replica_groups=mesh['dp'=16,'tensor'=2] {'dp'}, use_global_device_ids=true, to_apply=%region_11.12 | all-reduce | flops 13056 | bytes 104448 | tf_op jit(solution)/shard_map/psum | solution.py:368
  441.9 6.2 fusion.133
  451.6 3.8 copy.57
  455.5 10.1 %fusion.33 = f32[1,768,1536]{2,1,0:T(8,128)} fusion(bf16[32,64,768]{2,1,0:T(8,128)(2,1)} %copy-done.21, bf16[32,1,64,1536]{3,2,0,1:T(8,128)(2,1)} %copy-done.59), kind=kOutput, calls=%fused_computation.45 | convolution fusion | flops 4831838208 | bytes 14155776 | tf_op jit(solution)/shard_map/secd,secf->edf/dot_general | solution.py:346
  469.8 102.7 %all-reduce.7.cloned.1.call-done = bf16[768,3,384]{0,2,1:T(8,128)(2,1)} async-done(((bf16[768,3,384]{0,2,1:T(8,128)(2,1)}), bf16[768,3,384]{0,2,1:T(8,128)(2,1)}) %all-reduce.7.cloned.1.call-update) | async-done | bytes 1769488 | tf_op jit(solution)/shard_map/psum | solution.py:391
  572.5 4.0 copy.62
  576.5 4.0 fusion.41
  580.5 6.4 %fusion.40 = f32[1024,768]{0,1:T(8,128)} fusion(f32[1024,768]{0,1:T(8,128)} %get-tuple-element.72, bf16[1024,768]{0,1:T(8,128)(2,1)S(1)} %copy-done.15, f32[1024]{0:T(1024)S(1)} %broadcast_multiply_fusion, f32[768]{0:T(1024)S(1)} %copy-done.48, f32[1024]{0:T(1024)S(1)} %copy-done.46, f32[1024,768]{0,1:T(8,128)} %fusion.133, ...), kind=kLoop, calls=%fused_computation.52 | loop fusion | flops 6291456 | bytes 14167040 | tf_op jit(solution)/shard_map/add | solution.py:388
  590.4 41.0 %all-reduce = (f32[768]{0:T(1024)}, f32[32,6]{0,1:T(8,128)}) all-reduce(f32[768]{0:T(1024)S(1)} %get-tuple-element.62, f32[32,6]{0,1:T(8,128)S(1)} %fusion.106), channel_id=1, replica_groups=mesh['dp'=16,'tensor'=2] {'dp'}, use_global_device_ids=true, to_apply=%region_15.16 | all-reduce | flops 960 | bytes 7680 | tf_op jit(solution)/shard_map/psum | solution.py:392
  (188 shorter events, 71.2 us)
Async XLA Ops:
  7.2 148.0 %copy-start = (bf16[1,768,1536]{2,1,0:T(8,128)(2,1)S(1)}, bf16[1,768,1536]{2,1,0:T(8,128)(2,1)}, u32[]{:S(2)}) copy-start(bf16[1,768,1536]{2,1,0:T(8,128)(2,1)} %param.20) | copy-start | bytes 7077892
  22.3 25.1 %copy-start.2 = (bf16[1024,1152]{1,0:T(8,128)(2,1)}, bf16[1024,1152]{1,0:T(8,128)(2,1)S(1)}, u32[]{:S(2)}) copy-start(bf16[1024,1152]{1,0:T(8,128)(2,1)S(1)} %convolution_convert_fusion.q_ref.k_ref.v_ref) | copy-start | bytes 7077892
  22.3 26.0 %copy-start.18 = (bf16[384,768]{1,0:T(8,128)(2,1)S(1)}, bf16[384,768]{1,0:T(8,128)(2,1)}, u32[]{:S(2)}) copy-start(bf16[384,768]{1,0:T(8,128)(2,1)} %param.16) | copy-start | bytes 1769476
  51.0 6.1 collective-permute-start
  52.6 10.4 %copy-start.42 = (f32[768]{0:T(1024)S(1)}, f32[768]{0:T(1024)}, u32[]{:S(2)}) copy-start(f32[768]{0:T(1024)} %param.18) | copy-start | bytes 9220
  66.2 42.8 %all-to-all-start = ((bf16[16,64,768]{2,1,0:T(8,128)(2,1)}), bf16[16,64,768]{2,1,0:T(8,128)(2,1)}, u32[]{:S(2)}, u32[]{:S(2)}) async-start(bf16[16,64,768]{2,1,0:T(8,128)(2,1)} %bitcast.138), calls=%async_computation | async-start | bytes 3145728 | tf_op jit(solution)/shard_map/all_to_all | solution.py:237
  109.0 41.5 %all-to-all-start.2 = ((bf16[16,64,768]{2,1,0:T(8,128)(2,1)}), bf16[16,64,768]{2,1,0:T(8,128)(2,1)}, u32[]{:S(2)}, u32[]{:S(2)}) async-start(bf16[16,64,768]{2,1,0:T(8,128)(2,1)} %bitcast.137), calls=%async_computation.2 | async-start | bytes 3145728 | tf_op jit(solution)/shard_map/all_to_all | solution.py:237
  117.1 36.6 %collective-permute-start.1 = (bf16[16,64,768]{2,1,0:T(8,128)(2,1)}, bf16[16,64,768]{2,1,0:T(8,128)(2,1)}, u32[]{:S(2)}, u32[]{:S(2)}) collective-permute-start(bf16[16,64,768]{2,1,0:T(8,128)(2,1)} %all-to-all-done), channel_id=1, source_target_pairs={{0,1},{1,0},{2,3},{3,2},{4,5},{5,4},{6,7},{7,6},{8,9},{9,8},{10,11... | collective-permute-start | bytes 4718600 | tf_op jit(solution)/shard_map/ppermute | solution.py:228
  150.5 12.5 %collective-permute-start.4 = (bf16[16,64,768]{2,1,0:T(8,128)(2,1)}, bf16[16,64,768]{2,1,0:T(8,128)(2,1)S(1)}, u32[]{:S(2)}, u32[]{:S(2)}) collective-permute-start(bf16[16,64,768]{2,1,0:T(8,128)(2,1)} %all-to-all-done.2), channel_id=1, source_target_pairs={{0,1},{1,0},{2,3},{3,2},{4,5},{5,4},{6,7},{7,6},{8,9},{9,8},{10,11... | collective-permute-start | bytes 4718600 | tf_op jit(solution)/shard_map/ppermute | solution.py:228
  164.7 16.0 %copy-start.20 = (bf16[32,64,768]{2,1,0:T(8,128)(2,1)}, bf16[32,64,768]{2,1,0:T(8,128)(2,1)S(1)}, u32[]{:S(2)}) copy-start(bf16[32,64,768]{2,1,0:T(8,128)(2,1)S(1)} %constant_dynamic-update-slice_fusion.2) | copy-start | bytes 9437188
  186.2 3.6 collective-permute-start.5
  191.4 41.9 %all-to-all-start.3 = ((bf16[16,64,768]{2,1,0:T(8,128)(2,1)}), bf16[16,64,768]{2,1,0:T(8,128)(2,1)S(1)}, u32[]{:S(2)}, u32[]{:S(2)}) async-start(bf16[16,64,768]{2,1,0:T(8,128)(2,1)} %bitcast.40), calls=%async_computation.3 | async-start | bytes 3145728 | tf_op jit(solution)/shard_map/all_to_all | solution.py:237
  210.4 3.5 collective-permute-start.2
  215.4 26.3 %copy-start.52 = (f32[1024]{0:T(1024)S(1)}, f32[1024]{0:T(1024)}, u32[]{:S(2)}) copy-start(f32[1024]{0:T(1024)} %copy-done.51) | copy-start | bytes 12292
  215.4 26.9 %copy-start.31 = (s32[1024,1]{0,1:T(1,128)S(1)}, s32[1024,1]{0,1:T(1,128)}, u32[]{:S(2)}) copy-start(s32[1024,1]{0,1:T(1,128)} %param.22) | copy-start | bytes 12292
  233.3 42.2 %all-to-all-start.1 = ((bf16[16,64,768]{2,1,0:T(8,128)(2,1)}), bf16[16,64,768]{2,1,0:T(8,128)(2,1)}, u32[]{:S(2)}, u32[]{:S(2)}) async-start(bf16[16,64,768]{2,1,0:T(8,128)(2,1)} %bitcast.24), calls=%async_computation.1 | async-start | bytes 3145728 | tf_op jit(solution)/shard_map/all_to_all | solution.py:237
  241.6 200.2 %all-reduce.5.cloned.1.call-start = ((), (), s32[]{:S(2)}) async-start(), calls=%async_computation.4 | async-start | bytes 1179648 | tf_op jit(solution)/shard_map/psum | solution.py:368
  242.3 53.3 %collective-permute-start.6 = (bf16[1024,768]{1,0:T(8,128)(2,1)S(1)}, bf16[1024,768]{1,0:T(8,128)(2,1)}, u32[]{:S(2)}, u32[]{:S(2)}) collective-permute-start(bf16[1024,768]{1,0:T(8,128)(2,1)S(1)} %bitcast.135), channel_id=1, source_target_pairs={{0,1},{1,0},{2,3},{3,2},{4,5},{5,4},{6,7},{7,6},{8,9},{9,8},{10,11... | collective-permute-start | bytes 4718600 | tf_op jit(solution)/shard_map/ppermute | solution.py:228
  275.5 11.9 %copy-start.17 = (bf16[1024,768]{0,1:T(8,128)(2,1)S(1)}, bf16[1024,768]{0,1:T(8,128)(2,1)}, u32[]{:S(2)}) copy-start(bf16[1024,768]{0,1:T(8,128)(2,1)} %copy.51) | copy-start | bytes 4718596
  275.5 11.9 %collective-permute-start.3 = (bf16[1024,768]{1,0:T(8,128)(2,1)}, bf16[1024,768]{1,0:T(8,128)(2,1)S(1)}, u32[]{:S(2)}, u32[]{:S(2)}) collective-permute-start(bf16[1024,768]{1,0:T(8,128)(2,1)} %bitcast.25), channel_id=1, source_target_pairs={{0,1},{1,0},{2,3},{3,2},{4,5},{5,4},{6,7},{7,6},{8,9},{9,8},{10,11... | collective-permute-start | bytes 4718600 | tf_op jit(solution)/shard_map/ppermute | solution.py:228
  292.9 9.4 %copy-start.49 = (f32[1024]{0:T(1024)}, f32[1024]{0:T(1024)S(1)}, u32[]{:S(2)}) copy-start(f32[1024]{0:T(1024)S(1)} %get-tuple-element.76) | copy-start | bytes 12292
  312.3 260.1 %all-reduce.7.cloned.1.call-start = ((), (), s32[]{:S(2)}) async-start(), calls=%async_computation.5 | async-start | bytes 3538944 | tf_op jit(solution)/shard_map/psum | solution.py:391
  312.4 44.6 %copy-start.13 = (f32[1024,768]{0,1:T(8,128)S(1)}, f32[1024,768]{0,1:T(8,128)}, u32[]{:S(2)}) copy-start(f32[1024,768]{0,1:T(8,128)} %copy-done.11) | copy-start | bytes 9437188
  312.4 44.6 %copy-start.28 = (f32[1024]{0:T(1024)S(1)}, f32[1024]{0:T(1024)}, u32[]{:S(2)}) copy-start(f32[1024]{0:T(1024)} %copy-done.26) | copy-start | bytes 12292
  312.4 44.6 %copy-start.32 = (s32[1024,1]{0,1:T(1,128)S(1)}, s32[1024,1]{0,1:T(1,128)}, u32[]{:S(2)}) copy-start(s32[1024,1]{0,1:T(1,128)} %param.22) | copy-start | bytes 12292
  312.4 44.5 %copy-start.35 = (f32[1024]{0:T(1024)S(1)}, f32[1024]{0:T(1024)}, u32[]{:S(2)}) copy-start(f32[1024]{0:T(1024)} %copy-done.33) | copy-start | bytes 12292
  312.4 44.5 %copy-start.38 = (f32[1024]{0:T(1024)S(1)}, f32[1024]{0:T(1024)}, u32[]{:S(2)}) copy-start(f32[1024]{0:T(1024)} %copy-done.36) | copy-start | bytes 12292
  312.4 44.5 %copy-start.41 = (f32[1024]{0:T(1024)S(1)}, f32[1024]{0:T(1024)}, u32[]{:S(2)}) copy-start(f32[1024]{0:T(1024)} %copy-done.39) | copy-start | bytes 12292
  312.4 44.5 %copy-start.44 = (f32[768]{0:T(1024)S(1)}, f32[768]{0:T(1024)}, u32[]{:S(2)}) copy-start(f32[768]{0:T(1024)} %param.18) | copy-start | bytes 9220
  312.5 44.5 %copy-start.50 = (f32[1024]{0:T(1024)S(1)}, f32[1024]{0:T(1024)}, u32[]{:S(2)}) copy-start(f32[1024]{0:T(1024)} %copy-done.49) | copy-start | bytes 12292
  448.1 128.4 %collective-permute-start.7 = (f32[1024,768]{0,1:T(8,128)}, f32[1024,768]{0,1:T(8,128)}, u32[]{:S(2)}, u32[]{:S(2)}) collective-permute-start(f32[1024,768]{0,1:T(8,128)} %fusion.133), channel_id=1, source_target_pairs={{0,1},{1,0},{2,3},{3,2},{4,5},{5,4},{6,7},{7,6},{8,9},{9,8},{10,11... | collective-permute-start | bytes 9437192 | tf_op jit(solution)/shard_map/ppermute | solution.py:228
  580.5 51.0 %copy-start.1 = (bf16[1,768,1536]{2,1,0:T(8,128)(2,1)S(1)}, bf16[1,768,1536]{2,1,0:T(8,128)(2,1)}, u32[]{:S(2)}) copy-start(bf16[1,768,1536]{2,1,0:T(8,128)(2,1)} %param.20) | copy-start | bytes 7077892
  (42 other events, 155.8 us)
Sparse Core Ops, SparseCore 0:
  312.4 111.0 all-reduce.4
  455.6 116.8 all-reduce.6

commit v2 on v1

--- a/solution.py
+++ b/solution.py
@@ -182,6 +182,11 @@
         ],
         scratch_shapes=[pltpu.VMEM((2, ROWS, 2 * length - ROWS), jnp.float32)],
         compiler_params=pltpu.CompilerParams(vmem_limit_bytes=40 * 1024 * 1024),
+        cost_estimate=pl.CostEstimate(
+            flops=pairs * 2 * 2 * 2 * length * length * 128,
+            bytes_accessed=4 * pairs * length * 128 * 2,
+            transcendentals=pairs * 2 * length * length,
+        ),
         name="attention_forward",
     )(packed, packed, packed, segment_row[:, None], segment_row[None, :], bias_vec)
 
@@ -216,6 +221,11 @@
             pltpu.VMEM((length, 128), jnp.float32),
         ],
         compiler_params=pltpu.CompilerParams(vmem_limit_bytes=48 * 1024 * 1024),
+        cost_estimate=pl.CostEstimate(
+            flops=pairs * 2 * 5 * 2 * length * length * 128,
+            bytes_accessed=9 * pairs * length * 128 * 2,
+            transcendentals=pairs * 2 * length * length,
+        ),
         name="attention_backward",
     )(packed, packed, packed, out_grad, segment_row[:, None], segment_row[None, :], bias_vec, log_norm)
 
@@ -247,6 +257,18 @@
     summed = kept + swap(given.astype(jnp.bfloat16)).astype(jnp.float32)
     arrived = exchange(summed.astype(jnp.bfloat16), model_width).reshape(-1, model_width)
     return jnp.concatenate([arrived, swap(arrived)], axis=0)
+
+
+def all_to_all(shares):
+    return lax.all_to_all(shares, "dp", split_axis=0, concat_axis=0, tiled=True)
+
+
+def scatter_rows(values):
+    return values.reshape((lax.axis_size("dp"), -1) + values.shape[1:]).astype(jnp.bfloat16)
+
+
+def to_everyone(rows):
+    return jnp.broadcast_to(rows[None], (lax.axis_size("dp"),) + rows.shape).astype(jnp.bfloat16)
 
 
 def per_device(
@@ -278,6 +300,28 @@
     ).astype(jnp.float32)
     bias_vec = jnp.sum(near_hot[None] * bias_table.T[:, None, :], axis=2)
     bias_vec = bias_vec.reshape(heads_here // 2, 2, SPAN)
+    chosen = expert_ids[:, 0]
+    one_hot_int = (chosen[:, None] == jnp.arange(experts_all, dtype=jnp.int32)[None, :]).astype(
+        jnp.int32
+    )
+    one_hot_float = one_hot_int.astype(jnp.float32)
+    earlier = jnp.arange(length)[None, :] < jnp.arange(length)[:, None]
+    ranks = jnp.dot(
+        earlier.astype(jnp.bfloat16),
+        one_hot_float.astype(jnp.bfloat16),
+        preferred_element_type=jnp.float32,
+    )
+    slot_ids = jnp.sum(ranks * one_hot_float, axis=1).astype(jnp.int32)
+    side = (slot_ids >= half).astype(jnp.int32)
+    other_side = (side != lax.axis_index("tensor")).astype(jnp.int32)
+    target_rows = chosen * half + slot_ids - side * half + other_side * (experts_all * half)
+    own_slots = jnp.arange(experts_all * half, dtype=jnp.int32)
+    place = (own_slots[:, None] == target_rows[None, :]).astype(jnp.bfloat16)
+    all_slots = jnp.arange(2 * experts_all * half, dtype=jnp.int32)
+    pick = (target_rows[:, None] == all_slots[None, :]).astype(jnp.bfloat16)
+    upstream = cotangent.astype(jnp.float32)
+    cotangent_sent = jnp.dot(place, cotangent, preferred_element_type=jnp.float32)
+    cotangent_rows = to_owners(cotangent_sent.astype(jnp.bfloat16), model_width)
     inputs32 = tokens.astype(jnp.float32)
     scale_one = lax.rsqrt(jnp.mean(inputs32 * inputs32, axis=1, keepdims=True) + epsilon)
     normed_one = inputs32 * scale_one
@@ -294,36 +338,21 @@
     logit_peak = jnp.max(router_logits, axis=1, keepdims=True)
     router_exp = jnp.exp(router_logits - logit_peak)
     router_probs = router_exp / jnp.sum(router_exp, axis=1, keepdims=True)
-    chosen = expert_ids[:, 0]
-    one_hot_int = (chosen[:, None] == jnp.arange(experts_all, dtype=jnp.int32)[None, :]).astype(
-        jnp.int32
-    )
-    one_hot_float = one_hot_int.astype(jnp.float32)
     gate_prob = jnp.sum(router_probs * one_hot_float, axis=1)
-    earlier = jnp.arange(length)[None, :] < jnp.arange(length)[:, None]
-    ranks = jnp.dot(
-        earlier.astype(jnp.bfloat16),
-        one_hot_float.astype(jnp.bfloat16),
-        preferred_element_type=jnp.float32,
-    )
-    slot_ids = jnp.sum(ranks * one_hot_float, axis=1).astype(jnp.int32)
-    side = (slot_ids >= half).astype(jnp.int32)
-    other_side = (side != lax.axis_index("tensor")).astype(jnp.int32)
-    target_rows = chosen * half + slot_ids - side * half + other_side * (experts_all * half)
-    own_slots = jnp.arange(experts_all * half, dtype=jnp.int32)
-    place = (own_slots[:, None] == target_rows[None, :]).astype(jnp.bfloat16)
-    all_slots = jnp.arange(2 * experts_all * half, dtype=jnp.int32)
-    pick = (target_rows[:, None] == all_slots[None, :]).astype(jnp.bfloat16)
-    send_rows = jnp.dot(place, ffn_in.astype(jnp.bfloat16), preferred_element_type=jnp.float32)
-    expert_rows = to_owners(send_rows.astype(jnp.bfloat16), model_width).reshape(
-        -1, experts_here, half, model_width
-    )
-    upstream = cotangent.astype(jnp.float32)
-    back_rows = (gate_prob[:, None] * upstream).astype(jnp.bfloat16)
-    back_sent = jnp.dot(place, back_rows, preferred_element_type=jnp.float32)
-    expert_grads = to_owners(back_sent.astype(jnp.bfloat16), model_width).reshape(
-        -1, experts_here, half, model_width
-    )
+    gate_high = lax.reduce_precision(gate_prob, 8, 7)
+    gate_mid = lax.reduce_precision(gate_prob - gate_high, 8, 7)
+    gate_low = gate_prob - gate_high - gate_mid
+    gate_parts = jnp.stack([gate_high, gate_mid, gate_low], axis=1)
+    gate_parts = jnp.pad(gate_parts, ((0, 0), (0, 125))).astype(jnp.bfloat16)
+    sent = jnp.concatenate([ffn_in.astype(jnp.bfloat16), gate_parts], axis=1)
+    send_rows = jnp.dot(place, sent, preferred_element_type=jnp.float32)
+    arrived_rows = to_owners(send_rows.astype(jnp.bfloat16), model_width + 128)
+    expert_rows = arrived_rows[:, :, :model_width].reshape(-1, experts_here, half, model_width)
+    gate_rows = jnp.sum(
+        arrived_rows[:, :, model_width:].astype(jnp.float32), axis=2, keepdims=True
+    )
+    expert_grads = (gate_rows * cotangent_rows.astype(jnp.float32)).astype(jnp.bfloat16)
+    expert_grads = expert_grads.reshape(-1, experts_here, half, model_width)
     inner_act = jnp.einsum(
         "secd,edf->secf", expert_rows, expert_in, preferred_element_type=jnp.float32
     )
@@ -340,12 +369,6 @@
         "secd,efd->secf", expert_grads, expert_out, preferred_element_type=jnp.float32
     )
     grad_inner = gelu_back(grad_act)[0].astype(jnp.bfloat16)
-    grad_expert_out = jnp.einsum(
-        "secf,secd->efd", act_low, expert_grads, preferred_element_type=jnp.float32
-    )
-    grad_expert_in = jnp.einsum(
-        "secd,secf->edf", expert_rows, grad_inner, preferred_element_type=jnp.float32
-    )
     grad_rows = jnp.einsum(
         "secf,edf->secd", grad_inner, expert_in, preferred_element_type=jnp.float32
     )
@@ -365,9 +388,20 @@
     grad_mixed = jnp.dot(grad_attn, w_attn_out.T, preferred_element_type=jnp.float32).astype(
         jnp.bfloat16
     )
-    early = lax.psum(
-        (grad_w_attn_out.astype(jnp.bfloat16), grad_gain_ffn, grad_router), "dp"
-    )
+    share_rows = head_cols // lax.axis_size("dp")
+    early_sent = jnp.concatenate(
+        [
+            scatter_rows(grad_w_attn_out),
+            scatter_rows(grad_router.reshape(-1, model_width)),
+            to_everyone(grad_gain_ffn[None]),
+        ],
+        axis=1,
+    )
+    early_share = jnp.sum(all_to_all(early_sent).astype(jnp.float32), axis=0)
+    total_gain_ffn = early_share[-1]
+    early_all = all_to_all(to_everyone(early_share[:-1])).astype(jnp.float32)
+    total_attn_out = early_all[:, :share_rows].reshape(head_cols, model_width)
+    total_router = early_all[:, share_rows:].reshape(router.shape)
     grad_queries, grad_keys, grad_values, diagonals, far = attention_backward(
         packed, grad_mixed, segment_row, bias_vec, log_norm
     )
@@ -378,27 +412,41 @@
     grad_table = grad_table + jnp.where(bucket_row == half_count - 1, far[:, :1], 0.0)
     grad_table = grad_table + jnp.where(bucket_row == bucket_count - 1, far[:, 127:], 0.0)
     grad_packed = jnp.concatenate([grad_queries, grad_keys, grad_values], axis=1)
-    grad_packed, early = lax.optimization_barrier((grad_packed, early))
-    grad_w_qkv = jnp.dot(normed.T, grad_packed, preferred_element_type=jnp.float32).reshape(
-        model_width, 3, head_cols
-    )
+    grad_packed, late_grads, late_rows = lax.optimization_barrier(
+        (grad_packed, expert_grads, expert_rows)
+    )
+    grad_expert_out = jnp.einsum(
+        "secf,secd->efd", act_low, late_grads, preferred_element_type=jnp.float32
+    )
+    grad_expert_in = jnp.einsum(
+        "secd,secf->edf", late_rows, grad_inner, preferred_element_type=jnp.float32
+    )
+    grad_w_qkv = jnp.dot(normed.T, grad_packed, preferred_element_type=jnp.float32)
     grad_normed = heads_total(jnp.dot(grad_packed, w_flat.T, preferred_element_type=jnp.float32))
     grad_gain_attn = jnp.sum(grad_normed * normed_one, axis=0)
     grad_norm_one = grad_normed * gain_attn
     grad_tokens = grad_hidden + scale_one * (
         grad_norm_one - normed_one * jnp.mean(grad_norm_one * normed_one, axis=1, keepdims=True)
     )
-    total_w_qkv = lax.psum(grad_w_qkv.astype(jnp.bfloat16), "dp")
-    total_gain, total_table = lax.psum((grad_gain_attn, grad_table.T), "dp")
+    qkv_share = jnp.sum(all_to_all(scatter_rows(grad_w_qkv)).astype(jnp.float32), axis=0)
+    small = jnp.concatenate([grad_gain_attn, grad_table.T.reshape(-1)])
+    small = jnp.pad(small, (0, -small.shape[0] % (3 * head_cols))).reshape(-1, 3 * head_cols)
+    late_all = all_to_all(to_everyone(jnp.concatenate([qkv_share, small], axis=0)))
+    late_all = late_all.astype(jnp.float32)
+    total_w_qkv = late_all[:, : qkv_share.shape[0]].reshape(w_qkv.shape)
+    small_total = jnp.sum(late_all[:, qkv_share.shape[0] :], axis=0).reshape(-1)
+    total_gain = small_total[:model_width]
+    total_table = small_total[model_width : model_width + grad_table.size]
+    total_table = total_table.reshape(bias_table.shape)
     return (
         output,
         grad_tokens,
         total_gain,
-        total_w_qkv.astype(jnp.float32),
-        early[0].astype(jnp.float32),
+        total_w_qkv,
+        total_attn_out,
         total_table,
-        early[1],
-        early[2],
+        total_gain_ffn,
+        total_router,
         grad_expert_in,
         grad_expert_out,
     )

time: 648 us -> 507 us (0.78)
  the two profiles are of different devices: /device:TPU:0 before, /device:TPU:12 now
where the time goes in v2:
time: 507 us; the launch traced here: 500 us
  waiting for transfers between devices  194 us (38%)
  matrix products  106 us (21%)
  Pallas kernels  66.9 us (13%)
  local copies, waits for them, and re-layouts  54.5 us (11%)
  starting transfers between devices  44.5 us (9%)
  other arithmetic  32.8 us (6%)
    all_to_all x4, waiting for transfers between devices, exchange(): lax.all_to_all(grouped, 'dp', split_axis=0, concat_axis=0, tiled=True)  131 us
    all_to_all x4, waiting for transfers between devices, all_to_all(): return lax.all_to_all(shares, 'dp', split_axis=0, concat_axis=0, tiled=True)  54.7 us
    pallas_call x1, Pallas kernels, attention_backward(): pl.pallas_call(backward_kernel, grid=(pairs, length // ROWS), in_specs=[r...  41.7 us
    unnamed x75, local copies, waits for them, and re-layouts  28.8 us
    pallas_call x1, Pallas kernels, attention_forward(): pl.pallas_call(forward_kernel, grid=(pairs, length // ROWS), in_specs=[ro...  25.2 us
    all_to_all x4, starting transfers between devices, exchange(): lax.all_to_all(grouped, 'dp', split_axis=0, concat_axis=0, tiled=True)  22 us
    all_to_all x4, starting transfers between devices, all_to_all(): return lax.all_to_all(shares, 'dp', split_axis=0, concat_axis=0, tiled=True)  21.4 us
    dot_general x1, matrix products, per_device(): jnp.einsum('secd,efd->secf', expert_grads, expert_out, preferred_element_...  16.9 us
  transfers between devices with their start and end apart: 16, of which 9 were waited for; matrix products, arithmetic and copies ran while one was open for 25% of the time, Pallas kernels for 8%

profile of v2, /device:TPU:12, one launch (start us, length us, event | category | flops | bytes accessed | tf_op | source)
XLA Modules:
  0.0 500.3 jit_solution(15378244473332452694)
XLA Ops:
  10.3 4.4 convolution_convert_fusion.q_ref.k_ref.v_ref
  14.8 25.2 %attention_forward.1 = (bf16[1024,384]{1,0:T(8,128)(2,1)S(1)}, f32[1024,384]{1,0:T(8,128)S(1)}) custom-call(bf16[1024,1152]{1,0:T(8,128)(2,1)S(1)} %convolution_convert_fusion.q_ref.k_ref.v_ref, bf16[1024,1152]{1,0:T(8,128)(2,1)S(1)} %convolution_convert_fusion.q_ref.k_ref.v_ref, bf16[1024,1152]{1,0:T(8,128)(2,1)S(1)} %convolution_convert_fusion.q_ref.k_ref.v_ref, ...), custom_call_target="tpu_custom_call" | custom-call | flops 3221225472 | bytes 3145728 | tf_op jit(solution)/shard_map/attention_forward/pallas_call | solution.py:174
  44.5 5.5 %collective-permute-done = f32[1024,768]{0,1:T(8,128)} collective-permute-done((f32[1024,768]{0,1:T(8,128)}, f32[1024,768]{0,1:T(8,128)}, u32[]{:S(2)}, u32[]{:S(2)}) %collective-permute-start) | collective-permute-done | bytes 3145760 | tf_op jit(solution)/shard_map/ppermute | solution.py:238
  60.8 7.2 %all-to-all-start = ((bf16[16,64,896]{2,1,0:T(8,128)(2,1)}), bf16[16,64,896]{2,1,0:T(8,128)(2,1)}, u32[]{:S(2)}, u32[]{:S(2)}) async-start(bf16[16,64,896]{2,1,0:T(8,128)(2,1)} %bitcast.145), calls=%async_computation | async-start | bytes 3670016 | tf_op jit(solution)/shard_map/all_to_all | solution.py:247
  67.9 4.5 fusion.87
  72.4 38.4 %all-to-all-done = bf16[16,64,896]{2,1,0:T(8,128)(2,1)} async-done(((bf16[16,64,896]{2,1,0:T(8,128)(2,1)}), bf16[16,64,896]{2,1,0:T(8,128)(2,1)}, u32[]{:S(2)}, u32[]{:S(2)}) %all-to-all-start) | async-done | bytes 1835040 | tf_op jit(solution)/shard_map/all_to_all | solution.py:247
  110.8 5.2 %all-to-all-start.2 = ((bf16[16,64,768]{2,1,0:T(8,128)(2,1)}), bf16[16,64,768]{2,1,0:T(8,128)(2,1)}, u32[]{:S(2)}, u32[]{:S(2)}) async-start(bf16[16,64,768]{2,1,0:T(8,128)(2,1)} %bitcast.149), calls=%async_computation.2 | async-start | bytes 3145728 | tf_op jit(solution)/shard_map/all_to_all | solution.py:247
  116.1 36.4 %all-to-all-done.2 = bf16[16,64,768]{2,1,0:T(8,128)(2,1)} async-done(((bf16[16,64,768]{2,1,0:T(8,128)(2,1)}), bf16[16,64,768]{2,1,0:T(8,128)(2,1)}, u32[]{:S(2)}, u32[]{:S(2)}) %all-to-all-start.2) | async-done | bytes 1572896 | tf_op jit(solution)/shard_map/all_to_all | solution.py:247
  156.2 5.1 %fusion.58 = f32[32,64,1536]{2,1,0:T(8,128)S(1)} fusion(bf16[32,64,896]{2,1,0:T(8,128)(2,1)S(1)} %constant_dynamic-update-slice_fusion, bf16[1,768,1536]{2,1,0:T(8,128)(2,1)S(1)} %copy-done.29), kind=kOutput, calls=%fused_computation.80 | convolution fusion | flops 4831838208 | bytes 18087936 | tf_op jit(solution)/shard_map/secd,edf->secf/dot_general | solution.py:356
  161.3 7.7 %fusion.64 = f32[32,1,64,768]{3,2,0,1:T(8,128)S(1)} fusion(bf16[1,1536,768]{2,1,0:T(8,128)(2,1)S(1)} %copy-done, f32[32,64,1536]{2,1,0:T(8,128)S(1)} %fusion.58), kind=kOutput, calls=%fused_computation.87 | convolution fusion | flops 4860149760 | bytes 21233664 | tf_op jit(solution)/shard_map/secf,efd->secd/dot_general | solution.py:361
  172.7 16.9 %fusion.6 = bf16[32,1,64,1536]{3,2,0,1:T(8,128)(2,1)} fusion(f32[32,64,1536]{2,1,0:T(8,128)} %copy-done.31, bf16[16,64,768]{2,1,0:T(8,128)(2,1)S(1)} %collective-permute-done.4, bf16[16,64,768]{2,1,0:T(8,128)(2,1)} %all-to-all-done.2, f32[32,64]{1,0:T(8,128)S(1)} %convert_reduce_fusion.1, bf16[1,1536,768]{2,1,0:T(8,128)(2,1)S(1)} %copy-done), kind=kOutput, calls=%fused_computation.8 | convolution fusion | flops 4901044224 | bytes 24387584 | tf_op jit(solution)/shard_map/secd,efd->secf/dot_general | solution.py:368
  191.1 4.4 all-to-all-start.1
  195.6 7.2 %fusion.67 = f32[32,1,64,768]{3,2,0,1:T(8,128)S(1)} fusion(bf16[32,1,64,1536]{3,2,0,1:T(8,128)(2,1)} %fusion.6, bf16[1,768,1536]{2,1,0:T(8,128)(2,1)S(1)} %copy-done.30), kind=kOutput, calls=%fused_computation.88 | convolution fusion | flops 4831838208 | bytes 14942208 | tf_op jit(solution)/shard_map/secf,edf->secd/dot_general | solution.py:372
  208.1 24.8 %all-to-all-done.1 = bf16[16,64,768]{2,1,0:T(8,128)(2,1)} async-done(((bf16[16,64,768]{2,1,0:T(8,128)(2,1)}), bf16[16,64,768]{2,1,0:T(8,128)(2,1)}, u32[]{:S(2)}, u32[]{:S(2)}) %all-to-all-start.1) | async-done | bytes 1572896 | tf_op jit(solution)/shard_map/all_to_all | solution.py:247
  233.0 5.2 %all-to-all-start.3 = ((bf16[16,64,768]{2,1,0:T(8,128)(2,1)}), bf16[16,64,768]{2,1,0:T(8,128)(2,1)}, u32[]{:S(2)}, u32[]{:S(2)}) async-start(bf16[16,64,768]{2,1,0:T(8,128)(2,1)} %bitcast.41), calls=%async_computation.3 | async-start | bytes 3145728 | tf_op jit(solution)/shard_map/all_to_all | solution.py:247
  243.9 31.3 %all-to-all-done.3 = bf16[16,64,768]{2,1,0:T(8,128)(2,1)} async-done(((bf16[16,64,768]{2,1,0:T(8,128)(2,1)}), bf16[16,64,768]{2,1,0:T(8,128)(2,1)}, u32[]{:S(2)}, u32[]{:S(2)}) %all-to-all-start.3) | async-done | bytes 1572896 | tf_op jit(solution)/shard_map/all_to_all | solution.py:247
  278.7 6.0 %fusion.36 = (f32[1024]{0:T(1024)S(1)}, f32[1024,768]{0,1:T(8,128)S(1)}) fusion(bf16[1024,768]{0,1:T(8,128)(2,1)S(1)} %copy.72, bf16[1024,768]{1,0:T(8,128)(2,1)} %collective-permute-done.3, bf16[1024,768]{1,0:T(8,128)(2,1)} %bitcast.26, s32[1024]{0:T(1024)S(1)} %bitcast.161), kind=kOutput, calls=%fused_computation.49 | convolution fusion | flops 3231972352 | bytes 7872512 | tf_op jit(solution)/shard_map/dot_general | solution.py:365
  290.4 6.3 %multiply_reduce_fusion = (bf16[768]{0:T(1024)(128)(2,1)S(1)}, f32[1024]{0:T(1024)S(1)}, f32[1024,768]{0,1:T(8,128)S(1)}) fusion(f32[1024,768]{0,1:T(8,128)S(1)} %copy-done.9, f32[1024]{0:T(1024)S(1)} %add_rsqrt_fusion, f32[768]{0:T(1024)S(1)} %copy-done.26, f32[1024,768]{0,1:T(8,128)S(1)} %fusion.111, bf16[1024,768]{1,0:T(8,128)(2,1)S(1)} %collective-permute-done.6, ...), kind=kOutput, calls=%fused_computation.74 | convolution fusion | flops 3235117312 | bytes 12599808 | tf_op jit(solution)/shard_map/dot_general | solution.py:375
  304.8 4.3 all-to-all-start.6
  309.1 41.7 %attention_backward.1 = (bf16[1024,384]{1,0:T(8,128)(2,1)S(1)}, bf16[1024,384]{1,0:T(8,128)(2,1)S(1)}, bf16[1024,384]{1,0:T(8,128)(2,1)S(1)}, f32[3,2,512]{2,1,0:T(2,128)S(1)}, f32[3,2,128]{2,1,0:T(2,128)S(1)}) custom-call(bf16[1024,1152]{1,0:T(8,128)(2,1)} %copy-done.5, bf16[1024,1152]{1,0:T(8,128)(2,1)} %copy-done.5, bf16[1024,1152]{1,0:T(8,128)(2,1)} %copy-done.5, ...), custom_call_target="tpu_custom_call" | custom-call | flops 8053063680 | bytes 7077888 | tf_op jit(solution)/shard_map/attention_backward/pallas_call | solution.py:199
  356.3 6.9 %all-to-all-start.4 = ((bf16[16,48,1152]{2,1,0:T(8,128)(2,1)}), bf16[16,48,1152]{2,1,0:T(8,128)(2,1)}, u32[]{:S(2)}, u32[]{:S(2)}) async-start(bf16[16,48,1152]{2,1,0:T(8,128)(2,1)} %bitcast.148), calls=%async_computation.4 | async-start | bytes 3538944 | tf_op jit(solution)/shard_map/all_to_all | solution.py:263
  363.2 6.1 %fusion.155 = f32[1024,768]{0,1:T(8,128)} fusion(bf16[1024,1152]{1,0:T(8,128)(2,1)} %copy-done.20, bf16[768,1152]{0,1:T(8,128)(2,1)} %bitcast.147), kind=kOutput, calls=%fused_computation.205 | convolution fusion | flops 1811939328 | bytes 7274496 | tf_op jit(solution)/shard_map/dot_general | solution.py:425
  369.3 9.6 %fusion.33 = f32[1,768,1536]{2,1,0:T(8,128)} fusion(bf16[32,1,64,1536]{3,2,0,1:T(8,128)(2,1)} %fusion.6, bf16[32,1,64,768]{3,2,0,1:T(8,128)(2,1)} %slice_bitcast_fusion), kind=kOutput, calls=%fused_computation.46 | convolution fusion | flops 4831838208 | bytes 14155776 | tf_op jit(solution)/shard_map/secd,secf->edf/dot_general | solution.py:421
  380.2 24.4 %all-to-all-done.4 = bf16[16,48,1152]{2,1,0:T(8,128)(2,1)} async-done(((bf16[16,48,1152]{2,1,0:T(8,128)(2,1)}), bf16[16,48,1152]{2,1,0:T(8,128)(2,1)}, u32[]{:S(2)}, u32[]{:S(2)}) %all-to-all-start.4) | async-done | bytes 1769504 | tf_op jit(solution)/shard_map/all_to_all | solution.py:263
  405.6 4.8 all-to-all-start.7
  419.3 9.9 %all-to-all-done.7 = bf16[16,25,768]{2,1,0:T(8,128)(2,1)S(1)} async-done(((bf16[16,25,768]{2,1,0:T(8,128)(2,1)}), bf16[16,25,768]{2,1,0:T(8,128)(2,1)S(1)}, u32[]{:S(2)}, u32[]{:S(2)}) %all-to-all-start.7) | async-done | bytes 614432 | tf_op jit(solution)/shard_map/all_to_all | solution.py:263
  430.8 5.4 %all-to-all-start.5 = ((bf16[16,49,1152]{2,1,0:T(8,128)(2,1)}), bf16[16,49,1152]{2,1,0:T(8,128)(2,1)}, u32[]{:S(2)}, u32[]{:S(2)}) async-start(bf16[16,49,1152]{2,1,0:T(8,128)(2,1)} %broadcast_in_dim.48), calls=%async_computation.5 | async-start | bytes 4128768 | tf_op jit(solution)/shard_map/all_to_all | solution.py:263
  436.2 11.7 %fusion.30 = f32[1,1536,768]{2,1,0:T(8,128)} fusion(bf16[32,1,64,768]{3,2,0,1:T(8,128)(2,1)} %multiply_convert_fusion, f32[32,64,1536]{2,1,0:T(8,128)} %copy-done.31), kind=kOutput, calls=%fused_computation.45 | convolution fusion | flops 4860149760 | bytes 20447232 | tf_op jit(solution)/shard_map/secf,secd->efd/dot_general | solution.py:418
  453.4 5.4 %fusion.41 = f32[1024,768]{0,1:T(8,128)} fusion(f32[1024,768]{0,1:T(8,128)S(1)} %copy-done.11, bf16[1024,768]{0,1:T(8,128)(2,1)S(1)} %copy-done.13, f32[1024]{0:T(1024)S(1)} %broadcast_multiply_fusion, f32[768]{0:T(1024)S(1)} %copy-done.27, f32[1024]{0:T(1024)S(1)} %add_rsqrt_fusion.1, f32[1024,768]{0,1:T(8,128)} %fusion.155, ...), kind=kLoop, calls=%fused_computation.54 | loop fusion | flops 6291456 | bytes 14167040 | tf_op jit(solution)/shard_map/add | solution.py:428
  462.3 20.4 %all-to-all-done.5 = bf16[16,49,1152]{2,1,0:T(8,128)(2,1)} async-done(((bf16[16,49,1152]{2,1,0:T(8,128)(2,1)}), bf16[16,49,1152]{2,1,0:T(8,128)(2,1)}, u32[]{:S(2)}, u32[]{:S(2)}) %all-to-all-start.5) | async-done | bytes 1806368 | tf_op jit(solution)/shard_map/all_to_all | solution.py:263
  488.7 6.3 %reshape.417 = f32[768,3,384]{2,1,0:T(4,128)} reshape(f32[16,48,1152]{2,1,0:T(8,128)} %slice.64) | data formatting | bytes 7077888 | tf_op jit(solution)/shard_map/reshape | solution.py:436
  495.0 4.4 copy.85
  (164 shorter events, 95.9 us)
Async XLA Ops:
  0.6 160.6 %copy-start = (bf16[1,1536,768]{2,1,0:T(8,128)(2,1)S(1)}, bf16[1,1536,768]{2,1,0:T(8,128)(2,1)}, u32[]{:S(2)}) copy-start(bf16[1,1536,768]{2,1,0:T(8,128)(2,1)} %param.21) | copy-start | bytes 7077892
  3.5 5.8 %copy-start.4 = (s32[1,1024]{1,0:T(1,128)S(1)}, s32[1,1024]{1,0:T(1,128)}, u32[]{:S(2)}) copy-start(s32[1,1024]{1,0:T(1,128)} %seg_row.3) | copy-start | bytes 12292
  3.5 6.9 %copy-start.27 = (f32[768]{0:T(1024)S(1)}, f32[768]{0:T(1024)}, u32[]{:S(2)}) copy-start(f32[768]{0:T(1024)} %param.14) | copy-start | bytes 9220
  14.8 25.3 %copy-start.5 = (bf16[1024,1152]{1,0:T(8,128)(2,1)}, bf16[1024,1152]{1,0:T(8,128)(2,1)S(1)}, u32[]{:S(2)}) copy-start(bf16[1024,1152]{1,0:T(8,128)(2,1)S(1)} %convolution_convert_fusion.q_ref.k_ref.v_ref) | copy-start | bytes 7077892
  14.8 26.5 %copy-start.18 = (bf16[384,768]{1,0:T(8,128)(2,1)S(1)}, bf16[384,768]{1,0:T(8,128)(2,1)}, u32[]{:S(2)}) copy-start(bf16[384,768]{1,0:T(8,128)(2,1)} %param.16) | copy-start | bytes 1769476
  43.9 6.0 %collective-permute-start = (f32[1024,768]{0,1:T(8,128)}, f32[1024,768]{0,1:T(8,128)}, u32[]{:S(2)}, u32[]{:S(2)}) collective-permute-start(f32[1024,768]{0,1:T(8,128)} %fusion.154), channel_id=1, source_target_pairs={{0,1},{1,0},{2,3},{3,2},{4,5},{5,4},{6,7},{7,6},{8,9},{9,8},{10,11... | collective-permute-start | bytes 9437192 | tf_op jit(solution)/shard_map/ppermute | solution.py:238
  44.5 9.7 %copy-start.26 = (f32[768]{0:T(1024)S(1)}, f32[768]{0:T(1024)}, u32[]{:S(2)}) copy-start(f32[768]{0:T(1024)} %param.18) | copy-start | bytes 9220
  60.8 50.1 %all-to-all-start = ((bf16[16,64,896]{2,1,0:T(8,128)(2,1)}), bf16[16,64,896]{2,1,0:T(8,128)(2,1)}, u32[]{:S(2)}, u32[]{:S(2)}) async-start(bf16[16,64,896]{2,1,0:T(8,128)(2,1)} %bitcast.145), calls=%async_computation | async-start | bytes 3670016 | tf_op jit(solution)/shard_map/all_to_all | solution.py:247
  110.8 41.7 %all-to-all-start.2 = ((bf16[16,64,768]{2,1,0:T(8,128)(2,1)}), bf16[16,64,768]{2,1,0:T(8,128)(2,1)}, u32[]{:S(2)}, u32[]{:S(2)}) async-start(bf16[16,64,768]{2,1,0:T(8,128)(2,1)} %bitcast.149), calls=%async_computation.2 | async-start | bytes 3145728 | tf_op jit(solution)/shard_map/all_to_all | solution.py:247
  116.0 38.3 %collective-permute-start.1 = (bf16[16,64,896]{2,1,0:T(8,128)(2,1)}, bf16[16,64,896]{2,1,0:T(8,128)(2,1)}, u32[]{:S(2)}, u32[]{:S(2)}) collective-permute-start(bf16[16,64,896]{2,1,0:T(8,128)(2,1)} %all-to-all-done), channel_id=1, source_target_pairs={{0,1},{1,0},{2,3},{3,2},{4,5},{5,4},{6,7},{7,6},{8,9},{9,8},{10,11... | collective-permute-start | bytes 5505032 | tf_op jit(solution)/shard_map/ppermute | solution.py:238
  152.5 20.2 %collective-permute-start.4 = (bf16[16,64,768]{2,1,0:T(8,128)(2,1)}, bf16[16,64,768]{2,1,0:T(8,128)(2,1)S(1)}, u32[]{:S(2)}, u32[]{:S(2)}) collective-permute-start(bf16[16,64,768]{2,1,0:T(8,128)(2,1)} %all-to-all-done.2), channel_id=1, source_target_pairs={{0,1},{1,0},{2,3},{3,2},{4,5},{5,4},{6,7},{7,6},{8,9},{9,8},{10,11... | collective-permute-start | bytes 4718600 | tf_op jit(solution)/shard_map/ppermute | solution.py:238
  156.1 16.2 %copy-start.17 = (bf16[32,64,896]{2,1,0:T(8,128)(2,1)}, bf16[32,64,896]{2,1,0:T(8,128)(2,1)S(1)}, u32[]{:S(2)}) copy-start(bf16[32,64,896]{2,1,0:T(8,128)(2,1)S(1)} %constant_dynamic-update-slice_fusion) | copy-start | bytes 11010052
  161.3 7.7 %copy-start.31 = (f32[32,64,1536]{2,1,0:T(8,128)}, f32[32,64,1536]{2,1,0:T(8,128)S(1)}, u32[]{:S(2)}) copy-start(f32[32,64,1536]{2,1,0:T(8,128)S(1)} %fusion.58) | copy-start | bytes 37748740
  171.6 18.0 %collective-permute-start.2 = (bf16[1,1024,768]{2,1,0:T(8,128)(2,1)S(1)}, bf16[1,1024,768]{2,1,0:T(8,128)(2,1)S(1)}, u32[]{:S(2)}, u32[]{:S(2)}) collective-permute-start(bf16[1,1024,768]{2,1,0:T(8,128)(2,1)S(1)} %bitcast.150), channel_id=1, source_target_pairs={{0,1},{1,0},{2,3},{3,2},{4,5},{5,4},{6,7},{7,6},{8,9},{9,8},{10,11... | collective-permute-start | bytes 4718600 | tf_op jit(solution)/shard_map/ppermute | solution.py:238
  172.7 16.9 %slice-start = ((f32[32,1,64,768]{3,2,0,1:T(8,128)}), f32[16,1,64,768]{3,2,0,1:T(8,128)S(1)}, s32[]{:S(2)}) async-start(f32[32,1,64,768]{3,2,0,1:T(8,128)} %copy-done.14), calls=%async_computation.8 | async-start | bytes 6291456 | tf_op jit(solution)/shard_map/split | solution.py:256
  172.7 16.9 %copy-start.21 = (bf16[16,64,768]{2,1,0:T(8,128)(2,1)}, bf16[16,64,768]{2,1,0:T(8,128)(2,1)S(1)}, u32[]{:S(2)}) copy-start(bf16[16,64,768]{2,1,0:T(8,128)(2,1)S(1)} %collective-permute-done.4) | copy-start | bytes 4718596
  191.1 41.9 %all-to-all-start.1 = ((bf16[16,64,768]{2,1,0:T(8,128)(2,1)}), bf16[16,64,768]{2,1,0:T(8,128)(2,1)}, u32[]{:S(2)}, u32[]{:S(2)}) async-start(bf16[16,64,768]{2,1,0:T(8,128)(2,1)} %bitcast.25), calls=%async_computation.1 | async-start | bytes 3145728 | tf_op jit(solution)/shard_map/all_to_all | solution.py:247
  203.0 3.5 collective-permute-start.5
  233.0 42.2 %all-to-all-start.3 = ((bf16[16,64,768]{2,1,0:T(8,128)(2,1)}), bf16[16,64,768]{2,1,0:T(8,128)(2,1)}, u32[]{:S(2)}, u32[]{:S(2)}) async-start(bf16[16,64,768]{2,1,0:T(8,128)(2,1)} %bitcast.41), calls=%async_computation.3 | async-start | bytes 3145728 | tf_op jit(solution)/shard_map/all_to_all | solution.py:247
  238.2 40.5 %collective-permute-start.3 = (bf16[1024,768]{1,0:T(8,128)(2,1)}, bf16[1024,768]{1,0:T(8,128)(2,1)}, u32[]{:S(2)}, u32[]{:S(2)}) collective-permute-start(bf16[1024,768]{1,0:T(8,128)(2,1)} %bitcast.26), channel_id=1, source_target_pairs={{0,1},{1,0},{2,3},{3,2},{4,5},{5,4},{6,7},{7,6},{8,9},{9,8},{10,11... | collective-permute-start | bytes 4718600 | tf_op jit(solution)/shard_map/ppermute | solution.py:238
  275.2 15.2 %collective-permute-start.6 = (bf16[1024,768]{1,0:T(8,128)(2,1)}, bf16[1024,768]{1,0:T(8,128)(2,1)S(1)}, u32[]{:S(2)}, u32[]{:S(2)}) collective-permute-start(bf16[1024,768]{1,0:T(8,128)(2,1)} %bitcast.42), channel_id=1, source_target_pairs={{0,1},{1,0},{2,3},{3,2},{4,5},{5,4},{6,7},{7,6},{8,9},{9,8},{10,11... | collective-permute-start | bytes 4718600 | tf_op jit(solution)/shard_map/ppermute | solution.py:238
  278.7 6.0 %copy-start.9 = (f32[1024,768]{0,1:T(8,128)S(1)}, f32[1024,768]{0,1:T(8,128)}, u32[]{:S(2)}) copy-start(f32[1024,768]{0,1:T(8,128)} %copy-done.8) | copy-start | bytes 9437188
  300.6 8.6 %copy-start.3 = (s32[1024,1]{1,0:T(8,128)S(1)}, s32[1024,1]{1,0:T(8,128)}, u32[]{:S(2)}) copy-start(s32[1024,1]{1,0:T(8,128)} %copy.71.seg_col) | copy-start | bytes 12292
  302.3 6.9 %copy-start.7 = (f32[1024,384]{1,0:T(8,128)S(1)}, f32[1024,384]{1,0:T(8,128)}, u32[]{:S(2)}) copy-start(f32[1024,384]{1,0:T(8,128)} %copy-done.6) | copy-start | bytes 4718596
  304.8 51.5 %all-to-all-start.6 = ((bf16[16,26,768]{2,1,0:T(8,128)(2,1)}), bf16[16,26,768]{2,1,0:T(8,128)(2,1)}, u32[]{:S(2)}, u32[]{:S(2)}) async-start(bf16[16,26,768]{2,1,0:T(8,128)(2,1)} %pad_maximum_fusion.1), calls=%async_computation.6 | async-start | bytes 1572864 | tf_op jit(solution)/shard_map/all_to_all | solution.py:263
  356.3 48.3 %all-to-all-start.4 = ((bf16[16,48,1152]{2,1,0:T(8,128)(2,1)}), bf16[16,48,1152]{2,1,0:T(8,128)(2,1)}, u32[]{:S(2)}, u32[]{:S(2)}) async-start(bf16[16,48,1152]{2,1,0:T(8,128)(2,1)} %bitcast.148), calls=%async_computation.4 | async-start | bytes 3538944 | tf_op jit(solution)/shard_map/all_to_all | solution.py:263
  369.3 44.3 %collective-permute-start.7 = (f32[1024,768]{0,1:T(8,128)}, f32[1024,768]{0,1:T(8,128)}, u32[]{:S(2)}, u32[]{:S(2)}) collective-permute-start(f32[1024,768]{0,1:T(8,128)} %fusion.155), channel_id=1, source_target_pairs={{0,1},{1,0},{2,3},{3,2},{4,5},{5,4},{6,7},{7,6},{8,9},{9,8},{10,11... | collective-permute-start | bytes 9437192 | tf_op jit(solution)/shard_map/ppermute | solution.py:238
  378.9 31.7 %copy-start.23 = (f32[512,32]{0,1:T(8,128)S(1)}, f32[512,32]{0,1:T(8,128)}, u32[]{:S(2)}) copy-start(f32[512,32]{0,1:T(8,128)} %copy-done.22) | copy-start | bytes 196612
  405.6 23.6 %all-to-all-start.7 = ((bf16[16,25,768]{2,1,0:T(8,128)(2,1)}), bf16[16,25,768]{2,1,0:T(8,128)(2,1)S(1)}, u32[]{:S(2)}, u32[]{:S(2)}) async-start(bf16[16,25,768]{2,1,0:T(8,128)(2,1)} %broadcast_in_dim.50), calls=%async_computation.7 | async-start | bytes 1572864 | tf_op jit(solution)/shard_map/all_to_all | solution.py:263
  430.8 51.9 %all-to-all-start.5 = ((bf16[16,49,1152]{2,1,0:T(8,128)(2,1)}), bf16[16,49,1152]{2,1,0:T(8,128)(2,1)}, u32[]{:S(2)}, u32[]{:S(2)}) async-start(bf16[16,49,1152]{2,1,0:T(8,128)(2,1)} %broadcast_in_dim.48), calls=%async_computation.5 | async-start | bytes 4128768 | tf_op jit(solution)/shard_map/all_to_all | solution.py:263
  436.2 12.4 %copy-start.16 = (bf16[16,25,768]{2,1,0:T(8,128)(2,1)S(1)}, bf16[16,25,768]{2,1,0:T(8,128)(2,1)}, u32[]{:S(2)}) copy-start(bf16[16,25,768]{2,1,0:T(8,128)(2,1)} %copy-done.15) | copy-start | bytes 1843204
  488.7 11.4 %copy-start.1 = (bf16[1,1536,768]{2,1,0:T(8,128)(2,1)S(1)}, bf16[1,1536,768]{2,1,0:T(8,128)(2,1)}, u32[]{:S(2)}) copy-start(bf16[1,1536,768]{2,1,0:T(8,128)(2,1)} %param.21) | copy-start | bytes 7077892
  (17 other events, 46.4 us)

commit v3 on v2

--- a/solution.py
+++ b/solution.py
@@ -321,7 +321,7 @@
     pick = (target_rows[:, None] == all_slots[None, :]).astype(jnp.bfloat16)
     upstream = cotangent.astype(jnp.float32)
     cotangent_sent = jnp.dot(place, cotangent, preferred_element_type=jnp.float32)
-    cotangent_rows = to_owners(cotangent_sent.astype(jnp.bfloat16), model_width)
+    cotangent_arrived = exchange(cotangent_sent.astype(jnp.bfloat16), model_width)
     inputs32 = tokens.astype(jnp.float32)
     scale_one = lax.rsqrt(jnp.mean(inputs32 * inputs32, axis=1, keepdims=True) + epsilon)
     normed_one = inputs32 * scale_one
@@ -329,6 +329,8 @@
     w_flat = w_qkv.reshape(model_width, 3 * head_cols)
     packed = jnp.dot(normed, w_flat, preferred_element_type=jnp.float32).astype(jnp.bfloat16)
     mixed_heads, log_norm = attention_forward(packed, segment_row, bias_vec)
+    mixed_heads, cotangent_arrived = lax.optimization_barrier((mixed_heads, cotangent_arrived))
+    cotangent_rows = jnp.concatenate([cotangent_arrived, swap(cotangent_arrived)], axis=0)
     attn_part = jnp.dot(mixed_heads, w_attn_out, preferred_element_type=jnp.float32)
     hidden = inputs32 + heads_total(attn_part)
     scale_two = lax.rsqrt(jnp.mean(hidden * hidden, axis=1, keepdims=True) + epsilon)
@@ -399,9 +401,10 @@
     )
     early_share = jnp.sum(all_to_all(early_sent).astype(jnp.float32), axis=0)
     total_gain_ffn = early_share[-1]
-    early_all = all_to_all(to_everyone(early_share[:-1])).astype(jnp.float32)
-    total_attn_out = early_all[:, :share_rows].reshape(head_cols, model_width)
-    total_router = early_all[:, share_rows:].reshape(router.shape)
+    early_flat = early_share[:-1].reshape(-1)
+    early_size = early_flat.shape[0]
+    early_flat = jnp.pad(early_flat, (0, -early_size % (3 * head_cols)))
+    early_rows = early_flat.reshape(-1, 3 * head_cols)
     grad_queries, grad_keys, grad_values, diagonals, far = attention_backward(
         packed, grad_mixed, segment_row, bias_vec, log_norm
     )
@@ -428,13 +431,26 @@
     grad_tokens = grad_hidden + scale_one * (
         grad_norm_one - normed_one * jnp.mean(grad_norm_one * normed_one, axis=1, keepdims=True)
     )
-    qkv_share = jnp.sum(all_to_all(scatter_rows(grad_w_qkv)).astype(jnp.float32), axis=0)
+    qkv_sent = scatter_rows(grad_w_qkv)
+    qkv_rows = qkv_sent.shape[1]
+    late_sent = jnp.concatenate([qkv_sent, to_everyone(early_rows)], axis=1)
+    late_arrived = all_to_all(late_sent)
+    qkv_share = jnp.sum(late_arrived[:, :qkv_rows].astype(jnp.float32), axis=0)
+    early_all = late_arrived[:, qkv_rows:].reshape(late_arrived.shape[0], -1)[:, :early_size]
+    early_all = early_all.reshape(-1, share_rows + 1, model_width).astype(jnp.float32)
+    total_attn_out = early_all[:, :share_rows].reshape(head_cols, model_width)
+    total_router = early_all[:, share_rows:].reshape(router.shape)
     small = jnp.concatenate([grad_gain_attn, grad_table.T.reshape(-1)])
     small = jnp.pad(small, (0, -small.shape[0] % (3 * head_cols))).reshape(-1, 3 * head_cols)
     late_all = all_to_all(to_everyone(jnp.concatenate([qkv_share, small], axis=0)))
-    late_all = late_all.astype(jnp.float32)
-    total_w_qkv = late_all[:, : qkv_share.shape[0]].reshape(w_qkv.shape)
-    small_total = jnp.sum(late_all[:, qkv_share.shape[0] :], axis=0).reshape(-1)
+    qkv_parts = [
+        late_all[:, :qkv_rows, part * head_cols : (part + 1) * head_cols].reshape(
+            model_width, head_cols
+        )
+        for part in range(3)
+    ]
+    total_w_qkv = jnp.stack(qkv_parts, axis=1).astype(jnp.float32)
+    small_total = jnp.sum(late_all[:, qkv_rows:].astype(jnp.float32), axis=0).reshape(-1)
     total_gain = small_total[:model_width]
     total_table = small_total[model_width : model_width + grad_table.size]
     total_table = total_table.reshape(bias_table.shape)

time: 507 us -> 486 us (0.959)
  waiting for transfers between devices: 194 us -> 142 us
  blocking collectives: 0 us -> 49 us
  local copies, waits for them, and re-layouts: 54.5 us -> 42.8 us
  starting transfers between devices: 44.5 us -> 36.8 us
    all_to_all x4 -> x3, waiting for transfers between devices: 131 us -> 56.8 us  [exchange(): lax.all_to_all(grouped, 'dp', split_axis=0, concat_axis=0, tiled=True)]
    all_to_all x0 -> x1, blocking collectives: none -> 49 us  [exchange(): lax.all_to_all(grouped, 'dp', split_axis=0, concat_axis=0, tiled=True)]
    all_to_all x4 -> x3, waiting for transfers between devices: 54.7 us -> 70.8 us  [all_to_all(): return lax.all_to_all(shares, 'dp', split_axis=0, concat_axis=0, tiled=True)]
    reshape x1, local copies, waits for them, and re-layouts: 6.27 us -> 0.06 us  [per_device(): early_flat = early_share[:-1].reshape(-1)]
    ppermute x8, waiting for transfers between devices: 8.41 us -> 14 us  [swap(): return lax.ppermute(values, 'tensor', [(0, 1), (1, 0)])]
    unnamed x75 -> x71, local copies, waits for them, and re-layouts: 28.8 us -> 23.9 us
    all_to_all x4 -> x3, starting transfers between devices: 21.4 us -> 17.4 us  [all_to_all(): return lax.all_to_all(shares, 'dp', split_axis=0, concat_axis=0, tiled=True)]
    all_to_all x4 -> x3, starting transfers between devices: 22 us -> 18.6 us  [exchange(): lax.all_to_all(grouped, 'dp', split_axis=0, concat_axis=0, tiled=True)]
  transfers between devices with their start and end apart: 16 -> 14, of which waited for: 9 -> 8; matrix products, arithmetic and copies ran while one was open for 25% -> 28% of each run, Pallas kernels for 8% -> 5%
where the time goes in v3:
time: 486 us; the launch traced here: 478 us
  waiting for transfers between devices  142 us (29%)
  matrix products  105 us (22%)
  Pallas kernels  66.8 us (14%)
  blocking collectives  49 us (10%)
  local copies, waits for them, and re-layouts  42.8 us (9%)
  starting transfers between devices  36.8 us (8%)
  other arithmetic  34.2 us (7%)
    all_to_all x3, waiting for transfers between devices, all_to_all(): return lax.all_to_all(shares, 'dp', split_axis=0, concat_axis=0, tiled=True)  70.8 us
    all_to_all x3, waiting for transfers between devices, exchange(): lax.all_to_all(grouped, 'dp', split_axis=0, concat_axis=0, tiled=True)  56.8 us
    all_to_all x1, blocking collectives, exchange(): lax.all_to_all(grouped, 'dp', split_axis=0, concat_axis=0, tiled=True)  49 us
    pallas_call x1, Pallas kernels, attention_backward(): pl.pallas_call(backward_kernel, grid=(pairs, length // ROWS), in_specs=[r...  41.6 us
    pallas_call x1, Pallas kernels, attention_forward(): pl.pallas_call(forward_kernel, grid=(pairs, length // ROWS), in_specs=[ro...  25.2 us
    unnamed x71, local copies, waits for them, and re-layouts  23.9 us
    all_to_all x3, starting transfers between devices, exchange(): lax.all_to_all(grouped, 'dp', split_axis=0, concat_axis=0, tiled=True)  18.6 us
    all_to_all x3, starting transfers between devices, all_to_all(): return lax.all_to_all(shares, 'dp', split_axis=0, concat_axis=0, tiled=True)  17.4 us
  transfers between devices with their start and end apart: 14, of which 8 were waited for; matrix products, arithmetic and copies ran while one was open for 28% of the time, Pallas kernels for 5%

profile of v3, /device:TPU:12, one launch (start us, length us, event | category | flops | bytes accessed | tf_op | source)
XLA Modules:
  0.0 477.8 jit_solution(13311276841392676189)
XLA Ops:
  2.7 4.5 fusion.87
  7.2 7.2 %all-to-all-start = ((bf16[16,64,768]{2,1,0:T(8,128)(2,1)}), bf16[16,64,768]{2,1,0:T(8,128)(2,1)}, u32[]{:S(2)}, u32[]{:S(2)}) async-start(bf16[16,64,768]{2,1,0:T(8,128)(2,1)} %bitcast.159), calls=%async_computation | async-start | bytes 3145728 | tf_op jit(solution)/shard_map/all_to_all | solution.py:247
  17.0 3.9 copy.50
  24.5 4.4 convolution_convert_fusion.q_ref.k_ref.v_ref
  28.9 25.2 %attention_forward.1 = (bf16[1024,384]{1,0:T(8,128)(2,1)S(1)}, f32[1024,384]{1,0:T(8,128)S(1)}) custom-call(bf16[1024,1152]{1,0:T(8,128)(2,1)S(1)} %convolution_convert_fusion.q_ref.k_ref.v_ref, bf16[1024,1152]{1,0:T(8,128)(2,1)S(1)} %convolution_convert_fusion.q_ref.k_ref.v_ref, bf16[1024,1152]{1,0:T(8,128)(2,1)S(1)} %convolution_convert_fusion.q_ref.k_ref.v_ref, ...), custom_call_target="tpu_custom_call" | custom-call | flops 3221225472 | bytes 3145728 | tf_op jit(solution)/shard_map/attention_forward/pallas_call | solution.py:174
  59.0 5.6 %collective-permute-done = f32[1024,768]{0,1:T(8,128)S(1)} collective-permute-done((f32[1024,768]{0,1:T(8,128)S(1)}, f32[1024,768]{0,1:T(8,128)S(1)}, u32[]{:S(2)}, u32[]{:S(2)}) %collective-permute-start) | collective-permute-done | bytes 3145760 | tf_op jit(solution)/shard_map/ppermute | solution.py:238
  71.3 49.0 %all_to_all.35 = bf16[16,64,896]{2,1,0:T(8,128)(2,1)S(1)} all-to-all(bf16[16,64,896]{2,1,0:T(8,128)(2,1)S(1)} %bitcast.155), channel_id=1, replica_groups=mesh['dp'=16,'tensor'=2] {'dp'}, dimensions={0} | all-to-all | bytes 3670016 | tf_op jit(solution)/shard_map/all_to_all | solution.py:247
  121.0 5.4 %collective-permute-done.1 = bf16[16,64,896]{2,1,0:T(8,128)(2,1)S(1)} collective-permute-done((bf16[16,64,896]{2,1,0:T(8,128)(2,1)S(1)}, bf16[16,64,896]{2,1,0:T(8,128)(2,1)S(1)}, u32[]{:S(2)}, u32[]{:S(2)}) %collective-permute-start.1) | collective-permute-done | bytes 1835040 | tf_op jit(solution)/shard_map/ppermute | solution.py:238
  126.7 5.1 %fusion.58 = f32[32,64,1536]{2,1,0:T(8,128)S(1)} fusion(bf16[32,64,896]{2,1,0:T(8,128)(2,1)S(1)} %constant_dynamic-update-slice_fusion, bf16[1,768,1536]{2,1,0:T(8,128)(2,1)S(1)} %copy-done.27), kind=kOutput, calls=%fused_computation.80 | convolution fusion | flops 4831838208 | bytes 18087936 | tf_op jit(solution)/shard_map/secd,edf->secf/dot_general | solution.py:358
  131.8 7.7 %fusion.64 = f32[32,1,64,768]{3,2,0,1:T(8,128)S(1)} fusion(bf16[1,1536,768]{2,1,0:T(8,128)(2,1)S(1)} %copy-done, f32[32,64,1536]{2,1,0:T(8,128)S(1)} %fusion.58), kind=kOutput, calls=%fused_computation.87 | convolution fusion | flops 4860149760 | bytes 21233664 | tf_op jit(solution)/shard_map/secf,efd->secd/dot_general | solution.py:363
  143.0 16.5 %fusion.6 = bf16[32,1,64,1536]{3,2,0,1:T(8,128)(2,1)} fusion(f32[32,64,1536]{2,1,0:T(8,128)} %copy-done.29, bf16[16,64,768]{2,1,0:T(8,128)(2,1)} %collective-permute-done.4, bf16[16,64,768]{2,1,0:T(8,128)(2,1)} %all-to-all-done, f32[32,64]{1,0:T(8,128)S(1)} %convert_reduce_fusion.1, bf16[1,1536,768]{2,1,0:T(8,128)(2,1)S(1)} %copy-done), kind=kOutput, calls=%fused_computation.8 | convolution fusion | flops 4901044224 | bytes 24387584 | tf_op jit(solution)/shard_map/secd,efd->secf/dot_general | solution.py:370
  161.0 6.1 %all-to-all-start.2 = ((bf16[16,64,768]{2,1,0:T(8,128)(2,1)}), bf16[16,64,768]{2,1,0:T(8,128)(2,1)}, u32[]{:S(2)}, u32[]{:S(2)}) async-start(bf16[16,64,768]{2,1,0:T(8,128)(2,1)} %bitcast.26), calls=%async_computation.2 | async-start | bytes 3145728 | tf_op jit(solution)/shard_map/all_to_all | solution.py:247
  167.2 7.2 %fusion.67 = f32[32,1,64,768]{3,2,0,1:T(8,128)S(1)} fusion(bf16[32,1,64,1536]{3,2,0,1:T(8,128)(2,1)} %fusion.6, bf16[1,768,1536]{2,1,0:T(8,128)(2,1)S(1)} %copy-done.28), kind=kOutput, calls=%fused_computation.88 | convolution fusion | flops 4831838208 | bytes 14942208 | tf_op jit(solution)/shard_map/secf,edf->secd/dot_general | solution.py:374
  179.7 25.3 %all-to-all-done.2 = bf16[16,64,768]{2,1,0:T(8,128)(2,1)} async-done(((bf16[16,64,768]{2,1,0:T(8,128)(2,1)}), bf16[16,64,768]{2,1,0:T(8,128)(2,1)}, u32[]{:S(2)}, u32[]{:S(2)}) %all-to-all-start.2) | async-done | bytes 1572896 | tf_op jit(solution)/shard_map/all_to_all | solution.py:247
  205.0 5.2 %all-to-all-start.3 = ((bf16[16,64,768]{2,1,0:T(8,128)(2,1)}), bf16[16,64,768]{2,1,0:T(8,128)(2,1)}, u32[]{:S(2)}, u32[]{:S(2)}) async-start(bf16[16,64,768]{2,1,0:T(8,128)(2,1)} %bitcast.41), calls=%async_computation.3 | async-start | bytes 3145728 | tf_op jit(solution)/shard_map/all_to_all | solution.py:247
  212.0 3.9 slice_bitcast_fusion
  215.9 31.4 %all-to-all-done.3 = bf16[16,64,768]{2,1,0:T(8,128)(2,1)} async-done(((bf16[16,64,768]{2,1,0:T(8,128)(2,1)}), bf16[16,64,768]{2,1,0:T(8,128)(2,1)}, u32[]{:S(2)}, u32[]{:S(2)}) %all-to-all-start.3) | async-done | bytes 1572896 | tf_op jit(solution)/shard_map/all_to_all | solution.py:247
  247.4 3.6 multiply_convert_fusion
  251.0 6.0 %fusion.36 = (f32[1024]{0:T(1024)S(1)}, f32[1024,768]{0,1:T(8,128)S(1)}) fusion(bf16[1024,768]{0,1:T(8,128)(2,1)S(1)} %copy.52, bf16[1024,768]{1,0:T(8,128)(2,1)} %collective-permute-done.3, bf16[1024,768]{1,0:T(8,128)(2,1)} %bitcast.27, s32[1024]{0:T(1024)S(1)} %bitcast.170), kind=kOutput, calls=%fused_computation.49 | convolution fusion | flops 3231972352 | bytes 7872512 | tf_op jit(solution)/shard_map/dot_general | solution.py:367
  262.6 6.3 %multiply_reduce_fusion = (bf16[768]{0:T(1024)(128)(2,1)S(1)}, f32[1024]{0:T(1024)S(1)}, f32[1024,768]{0,1:T(8,128)S(1)}) fusion(f32[1024,768]{0,1:T(8,128)S(1)} %copy-done.9, f32[1024]{0:T(1024)S(1)} %add_rsqrt_fusion, f32[768]{0:T(1024)S(1)} %copy-done.24, f32[1024,768]{0,1:T(8,128)S(1)} %fusion.112, bf16[1024,768]{1,0:T(8,128)(2,1)S(1)} %collective-permute-done.6, ...), kind=kOutput, calls=%fused_computation.74 | convolution fusion | flops 3235117312 | bytes 12599808 | tf_op jit(solution)/shard_map/dot_general | solution.py:377
  274.0 41.6 %attention_backward.1 = (bf16[1024,384]{1,0:T(8,128)(2,1)S(1)}, bf16[1024,384]{1,0:T(8,128)(2,1)S(1)}, bf16[1024,384]{1,0:T(8,128)(2,1)S(1)}, f32[3,2,512]{2,1,0:T(2,128)S(1)}, f32[3,2,128]{2,1,0:T(2,128)S(1)}) custom-call(bf16[1024,1152]{1,0:T(8,128)(2,1)} %copy-done.5, bf16[1024,1152]{1,0:T(8,128)(2,1)} %copy-done.5, bf16[1024,1152]{1,0:T(8,128)(2,1)} %copy-done.5, ...), custom_call_target="tpu_custom_call" | custom-call | flops 8053063680 | bytes 7077888 | tf_op jit(solution)/shard_map/attention_backward/pallas_call | solution.py:199
  318.6 4.9 %all-to-all-start.4 = ((bf16[16,26,768]{2,1,0:T(8,128)(2,1)}), bf16[16,26,768]{2,1,0:T(8,128)(2,1)S(1)}, u32[]{:S(2)}, u32[]{:S(2)}) async-start(bf16[16,26,768]{2,1,0:T(8,128)(2,1)} %pad_maximum_fusion.2), calls=%async_computation.4 | async-start | bytes 1572864 | tf_op jit(solution)/shard_map/all_to_all | solution.py:263
  323.5 9.6 %fusion.33 = f32[1,768,1536]{2,1,0:T(8,128)} fusion(bf16[32,1,64,1536]{3,2,0,1:T(8,128)(2,1)} %fusion.6, bf16[32,1,64,768]{3,2,0,1:T(8,128)(2,1)} %slice_bitcast_fusion), kind=kOutput, calls=%fused_computation.46 | convolution fusion | flops 4831838208 | bytes 14155776 | tf_op jit(solution)/shard_map/secd,secf->edf/dot_general | solution.py:424
  333.2 6.2 %fusion.157 = f32[1024,768]{0,1:T(8,128)} fusion(bf16[1024,1152]{1,0:T(8,128)(2,1)} %pad_maximum_fusion.1, bf16[768,1152]{0,1:T(8,128)(2,1)} %bitcast.157), kind=kOutput, calls=%fused_computation.211 | convolution fusion | flops 1811939328 | bytes 7274496 | tf_op jit(solution)/shard_map/dot_general | solution.py:428
  347.3 6.6 %all-to-all-start.5 = ((bf16[16,65,1152]{2,1,0:T(8,128)(2,1)}), bf16[16,65,1152]{2,1,0:T(8,128)(2,1)}, u32[]{:S(2)}, u32[]{:S(2)}) async-start(bf16[16,65,1152]{2,1,0:T(8,128)(2,1)} %pad_maximum_fusion), calls=%async_computation.5 | async-start | bytes 5308416 | tf_op jit(solution)/shard_map/all_to_all | solution.py:263
  357.1 11.7 %fusion.30 = f32[1,1536,768]{2,1,0:T(8,128)} fusion(bf16[32,1,64,768]{3,2,0,1:T(8,128)(2,1)} %multiply_convert_fusion, f32[32,64,1536]{2,1,0:T(8,128)} %copy-done.29), kind=kOutput, calls=%fused_computation.45 | convolution fusion | flops 4860149760 | bytes 20447232 | tf_op jit(solution)/shard_map/secf,secd->efd/dot_general | solution.py:421
  369.4 4.0 fusion.42
  373.5 5.4 %fusion.41 = f32[1024,768]{0,1:T(8,128)} fusion(f32[1024,768]{0,1:T(8,128)S(1)} %copy-done.11, bf16[1024,768]{0,1:T(8,128)(2,1)S(1)} %copy-done.13, f32[1024]{0:T(1024)S(1)} %broadcast_multiply_fusion, f32[768]{0:T(1024)S(1)} %copy-done.25, f32[1024]{0:T(1024)S(1)} %add_rsqrt_fusion.1, f32[1024,768]{0,1:T(8,128)} %fusion.157, ...), kind=kLoop, calls=%fused_computation.54 | loop fusion | flops 6291456 | bytes 14167040 | tf_op jit(solution)/shard_map/add | solution.py:431
  378.9 3.5 copy.64
  382.4 32.2 %all-to-all-done.5 = bf16[16,65,1152]{2,1,0:T(8,128)(2,1)} async-done(((bf16[16,65,1152]{2,1,0:T(8,128)(2,1)}), bf16[16,65,1152]{2,1,0:T(8,128)(2,1)}, u32[]{:S(2)}, u32[]{:S(2)}) %all-to-all-start.5) | async-done | bytes 2396192 | tf_op jit(solution)/shard_map/all_to_all | solution.py:263
  417.8 5.9 %all-to-all-start.6 = ((bf16[16,49,1152]{2,1,0:T(8,128)(2,1)}), bf16[16,49,1152]{2,1,0:T(8,128)(2,1)S(1)}, u32[]{:S(2)}, u32[]{:S(2)}) async-start(bf16[16,49,1152]{2,1,0:T(8,128)(2,1)} %broadcast_in_dim.50), calls=%async_computation.6 | async-start | bytes 4128768 | tf_op jit(solution)/shard_map/all_to_all | solution.py:263
  433.3 37.8 %all-to-all-done.6 = bf16[16,49,1152]{2,1,0:T(8,128)(2,1)S(1)} async-done(((bf16[16,49,1152]{2,1,0:T(8,128)(2,1)}), bf16[16,49,1152]{2,1,0:T(8,128)(2,1)S(1)}, u32[]{:S(2)}, u32[]{:S(2)}) %all-to-all-start.6) | async-done | bytes 1806368 | tf_op jit(solution)/shard_map/all_to_all | solution.py:263
  (162 shorter events, 77.2 us)
Async XLA Ops:
  0.6 131.2 %copy-start = (bf16[1,1536,768]{2,1,0:T(8,128)(2,1)S(1)}, bf16[1,1536,768]{2,1,0:T(8,128)(2,1)}, u32[]{:S(2)}) copy-start(bf16[1,1536,768]{2,1,0:T(8,128)(2,1)} %param.21) | copy-start | bytes 7077892
  7.2 49.5 %all-to-all-start = ((bf16[16,64,768]{2,1,0:T(8,128)(2,1)}), bf16[16,64,768]{2,1,0:T(8,128)(2,1)}, u32[]{:S(2)}, u32[]{:S(2)}) async-start(bf16[16,64,768]{2,1,0:T(8,128)(2,1)} %bitcast.159), calls=%async_computation | async-start | bytes 3145728 | tf_op jit(solution)/shard_map/all_to_all | solution.py:247
  14.4 7.1 %copy-start.26 = (f32[32,6]{0,1:T(8,128)S(1)}, f32[32,6]{0,1:T(8,128)}, u32[]{:S(2)}) copy-start(f32[32,6]{0,1:T(8,128)} %param.17) | copy-start | bytes 2308
  14.4 7.2 %copy-start.4 = (s32[1,1024]{1,0:T(1,128)S(1)}, s32[1,1024]{1,0:T(1,128)}, u32[]{:S(2)}) copy-start(s32[1,1024]{1,0:T(1,128)} %seg_row.3) | copy-start | bytes 12292
  17.0 7.5 %copy-start.25 = (f32[768]{0:T(1024)S(1)}, f32[768]{0:T(1024)}, u32[]{:S(2)}) copy-start(f32[768]{0:T(1024)} %param.14) | copy-start | bytes 9220
  24.5 4.4 copy-start.2
  56.7 8.0 %copy-start.12 = (bf16[1024,768]{0,1:T(8,128)(2,1)S(1)}, bf16[1024,768]{0,1:T(8,128)(2,1)}, u32[]{:S(2)}) copy-start(bf16[1024,768]{0,1:T(8,128)(2,1)} %copy.49) | copy-start | bytes 4718596
  58.9 7.0 %copy-start.24 = (f32[768]{0:T(1024)S(1)}, f32[768]{0:T(1024)}, u32[]{:S(2)}) copy-start(f32[768]{0:T(1024)} %param.18) | copy-start | bytes 9220
  58.9 5.7 %collective-permute-start = (f32[1024,768]{0,1:T(8,128)S(1)}, f32[1024,768]{0,1:T(8,128)S(1)}, u32[]{:S(2)}, u32[]{:S(2)}) collective-permute-start(f32[1024,768]{0,1:T(8,128)S(1)} %fusion.156), channel_id=1, source_target_pairs={{0,1},{1,0},{2,3},{3,2},{4,5},{5,4},{6,7},{7,6},{8,9},{9,8},{10,11... | collective-permute-start | bytes 9437192 | tf_op jit(solution)/shard_map/ppermute | solution.py:238
  120.3 6.3 %copy-start.27 = (bf16[1,768,1536]{2,1,0:T(8,128)(2,1)S(1)}, bf16[1,768,1536]{2,1,0:T(8,128)(2,1)}, u32[]{:S(2)}) copy-start(bf16[1,768,1536]{2,1,0:T(8,128)(2,1)} %param.20) | copy-start | bytes 7077892
  120.3 6.0 %collective-permute-start.1 = (bf16[16,64,896]{2,1,0:T(8,128)(2,1)S(1)}, bf16[16,64,896]{2,1,0:T(8,128)(2,1)S(1)}, u32[]{:S(2)}, u32[]{:S(2)}) collective-permute-start(bf16[16,64,896]{2,1,0:T(8,128)(2,1)S(1)} %all_to_all.35), channel_id=1, source_target_pairs={{0,1},{1,0},{2,3},{3,2},{4,5},{5,4},{6,7},{7,6},{8,9},{9,8},{10,11... | collective-permute-start | bytes 5505032 | tf_op jit(solution)/shard_map/ppermute | solution.py:238
  120.3 22.7 %collective-permute-start.4 = (bf16[16,64,768]{2,1,0:T(8,128)(2,1)}, bf16[16,64,768]{2,1,0:T(8,128)(2,1)}, u32[]{:S(2)}, u32[]{:S(2)}) collective-permute-start(bf16[16,64,768]{2,1,0:T(8,128)(2,1)} %all-to-all-done), channel_id=1, source_target_pairs={{0,1},{1,0},{2,3},{3,2},{4,5},{5,4},{6,7},{7,6},{8,9},{9,8},{10,11... | collective-permute-start | bytes 4718600 | tf_op jit(solution)/shard_map/ppermute | solution.py:238
  126.7 15.9 %copy-start.15 = (bf16[32,64,896]{2,1,0:T(8,128)(2,1)}, bf16[32,64,896]{2,1,0:T(8,128)(2,1)S(1)}, u32[]{:S(2)}) copy-start(bf16[32,64,896]{2,1,0:T(8,128)(2,1)S(1)} %constant_dynamic-update-slice_fusion) | copy-start | bytes 11010052
  131.8 7.7 %copy-start.29 = (f32[32,64,1536]{2,1,0:T(8,128)}, f32[32,64,1536]{2,1,0:T(8,128)S(1)}, u32[]{:S(2)}) copy-start(f32[32,64,1536]{2,1,0:T(8,128)S(1)} %fusion.58) | copy-start | bytes 37748740
  142.1 17.4 %collective-permute-start.2 = (bf16[1,1024,768]{2,1,0:T(8,128)(2,1)S(1)}, bf16[1,1024,768]{2,1,0:T(8,128)(2,1)S(1)}, u32[]{:S(2)}, u32[]{:S(2)}) collective-permute-start(bf16[1,1024,768]{2,1,0:T(8,128)(2,1)S(1)} %bitcast.160), channel_id=1, source_target_pairs={{0,1},{1,0},{2,3},{3,2},{4,5},{5,4},{6,7},{7,6},{8,9},{9,8},{10,11... | collective-permute-start | bytes 4718600 | tf_op jit(solution)/shard_map/ppermute | solution.py:238
  143.0 16.5 %slice-start = ((f32[32,1,64,768]{3,2,0,1:T(8,128)}), f32[16,1,64,768]{3,2,0,1:T(8,128)S(1)}, s32[]{:S(2)}) async-start(f32[32,1,64,768]{3,2,0,1:T(8,128)} %copy-done.14), calls=%async_computation.7 | async-start | bytes 6291456 | tf_op jit(solution)/shard_map/split | solution.py:256
  161.0 6.1 %copy-start.28 = (bf16[1,768,1536]{2,1,0:T(8,128)(2,1)S(1)}, bf16[1,768,1536]{2,1,0:T(8,128)(2,1)}, u32[]{:S(2)}) copy-start(bf16[1,768,1536]{2,1,0:T(8,128)(2,1)} %param.20) | copy-start | bytes 7077892
  161.0 44.0 %all-to-all-start.2 = ((bf16[16,64,768]{2,1,0:T(8,128)(2,1)}), bf16[16,64,768]{2,1,0:T(8,128)(2,1)}, u32[]{:S(2)}, u32[]{:S(2)}) async-start(bf16[16,64,768]{2,1,0:T(8,128)(2,1)} %bitcast.26), calls=%async_computation.2 | async-start | bytes 3145728 | tf_op jit(solution)/shard_map/all_to_all | solution.py:247
  174.6 3.5 collective-permute-start.5
  205.0 42.4 %all-to-all-start.3 = ((bf16[16,64,768]{2,1,0:T(8,128)(2,1)}), bf16[16,64,768]{2,1,0:T(8,128)(2,1)}, u32[]{:S(2)}, u32[]{:S(2)}) async-start(bf16[16,64,768]{2,1,0:T(8,128)(2,1)} %bitcast.41), calls=%async_computation.3 | async-start | bytes 3145728 | tf_op jit(solution)/shard_map/all_to_all | solution.py:247
  210.2 40.7 %collective-permute-start.3 = (bf16[1024,768]{1,0:T(8,128)(2,1)}, bf16[1024,768]{1,0:T(8,128)(2,1)}, u32[]{:S(2)}, u32[]{:S(2)}) collective-permute-start(bf16[1024,768]{1,0:T(8,128)(2,1)} %bitcast.27), channel_id=1, source_target_pairs={{0,1},{1,0},{2,3},{3,2},{4,5},{5,4},{6,7},{7,6},{8,9},{9,8},{10,11... | collective-permute-start | bytes 4718600 | tf_op jit(solution)/shard_map/ppermute | solution.py:238
  247.4 15.3 %collective-permute-start.6 = (bf16[1024,768]{1,0:T(8,128)(2,1)}, bf16[1024,768]{1,0:T(8,128)(2,1)S(1)}, u32[]{:S(2)}, u32[]{:S(2)}) collective-permute-start(bf16[1024,768]{1,0:T(8,128)(2,1)} %bitcast.42), channel_id=1, source_target_pairs={{0,1},{1,0},{2,3},{3,2},{4,5},{5,4},{6,7},{7,6},{8,9},{9,8},{10,11... | collective-permute-start | bytes 4718600 | tf_op jit(solution)/shard_map/ppermute | solution.py:238
  251.0 6.0 %copy-start.9 = (f32[1024,768]{0,1:T(8,128)S(1)}, f32[1024,768]{0,1:T(8,128)}, u32[]{:S(2)}) copy-start(f32[1024,768]{0,1:T(8,128)} %copy-done.8) | copy-start | bytes 9437188
  318.6 25.1 %all-to-all-start.4 = ((bf16[16,26,768]{2,1,0:T(8,128)(2,1)}), bf16[16,26,768]{2,1,0:T(8,128)(2,1)S(1)}, u32[]{:S(2)}, u32[]{:S(2)}) async-start(bf16[16,26,768]{2,1,0:T(8,128)(2,1)} %pad_maximum_fusion.2), calls=%async_computation.4 | async-start | bytes 1572864 | tf_op jit(solution)/shard_map/all_to_all | solution.py:263
  333.2 6.3 %copy-start.13 = (bf16[1024,768]{0,1:T(8,128)(2,1)S(1)}, bf16[1024,768]{0,1:T(8,128)(2,1)}, u32[]{:S(2)}) copy-start(bf16[1024,768]{0,1:T(8,128)(2,1)} %copy.49) | copy-start | bytes 4718596
  333.2 6.3 %copy-start.19 = (bf16[1024,1152]{1,0:T(8,128)(2,1)S(1)}, bf16[1024,1152]{1,0:T(8,128)(2,1)}, u32[]{:S(2)}) copy-start(bf16[1024,1152]{1,0:T(8,128)(2,1)} %pad_maximum_fusion.1) | copy-start | bytes 7077892
  339.4 30.0 %collective-permute-start.7 = (f32[1024,768]{0,1:T(8,128)}, f32[1024,768]{0,1:T(8,128)}, u32[]{:S(2)}, u32[]{:S(2)}) collective-permute-start(f32[1024,768]{0,1:T(8,128)} %fusion.157), channel_id=1, source_target_pairs={{0,1},{1,0},{2,3},{3,2},{4,5},{5,4},{6,7},{7,6},{8,9},{9,8},{10,11... | collective-permute-start | bytes 9437192 | tf_op jit(solution)/shard_map/ppermute | solution.py:238
  347.3 6.9 %copy-start.21 = (f32[512,32]{0,1:T(8,128)S(1)}, f32[512,32]{0,1:T(8,128)}, u32[]{:S(2)}) copy-start(f32[512,32]{0,1:T(8,128)} %copy-done.20) | copy-start | bytes 196612
  347.3 67.4 %all-to-all-start.5 = ((bf16[16,65,1152]{2,1,0:T(8,128)(2,1)}), bf16[16,65,1152]{2,1,0:T(8,128)(2,1)}, u32[]{:S(2)}, u32[]{:S(2)}) async-start(bf16[16,65,1152]{2,1,0:T(8,128)(2,1)} %pad_maximum_fusion), calls=%async_computation.5 | async-start | bytes 5308416 | tf_op jit(solution)/shard_map/all_to_all | solution.py:263
  369.4 4.0 copy-start.11
  417.8 53.2 %all-to-all-start.6 = ((bf16[16,49,1152]{2,1,0:T(8,128)(2,1)}), bf16[16,49,1152]{2,1,0:T(8,128)(2,1)S(1)}, u32[]{:S(2)}, u32[]{:S(2)}) async-start(bf16[16,49,1152]{2,1,0:T(8,128)(2,1)} %broadcast_in_dim.50), calls=%async_computation.6 | async-start | bytes 4128768 | tf_op jit(solution)/shard_map/all_to_all | solution.py:263
  473.8 3.8 copy-start.1
  (13 other events, 24.2 us)
